TPU v7x, 128 devices: a whole 4x4x4 slice. The times are simulated.
128 devices in a mesh: hi: 4 (over z_hi, core), lo: 32 (over y, x, z_lo).
Axes of the slice: x: 4, y: 4, z: 4 (z_hi: 2, z_lo: 2; z = z_hi * 2 + z_lo), core: 2. Of those that a mesh axis runs over, the one named last changes fastest.
Arguments:
- src_position: float32 [16384, 2, 128], P(('hi', 'lo')), may hold values from -1 to 1
- src_weight: float32 [16384, 2, 128], P(('hi', 'lo')), may hold values from -6 to 6
- src_phase: float32 [16384, 128], P(('hi', 'lo')), may hold values from -3.140625 to 3.140625
- block_box: int32 [16384], P(('hi', 'lo')), may hold values from 0 to 32767
- block_count: int32 [128], P(('hi', 'lo')), may hold values from 1 to 128, as said below
- node_rate: float32 [32768, 64], P(('hi', 'lo')), may hold values from -3.140625 to 3.140625
- target_phase: float32 [32768, 256], P(('hi', 'lo')), may hold values from -3.140625 to 3.140625
Outputs:
- target_field: float32 [2, 32768, 256], P(None, ('hi', 'lo'))
Inputs may be any that keep to these rules, and one draw needn't show every extreme that they name: `block_count`: every device has at least one live block, and some device has all 128 live.
All inputs are finite; a program needn't handle non-finite values.
Results may differ from a plain program's by a relative error of at most 0.0003.
Values sent between devices are 32-bit elements; how exact they have to be, the bound alone decides.
A program may use at most 128 MiB of HBM per device.

v0:
```python
import math

import jax
import jax.numpy as jnp
from jax import lax
from jax.sharding import PartitionSpec as P

HIGH = lax.Precision.HIGHEST


def partner_2(value, axis, distance):
    mask = 2**distance
    pairs = [(source, source ^ mask) for source in range(lax.axis_size(axis))]
    return lax.ppermute(value, axis, pairs)


def cheb_nodes():
    order = jnp.arange(8).astype(jnp.float32)
    return jnp.cos((2.0 * order + 1.0) * math.pi / 16.0)


def lagrange(points):
    nodes = cheb_nodes()
    columns = []
    for index in range(8):
        value = jnp.ones_like(points)
        for other in range(8):
            if other != index:
                value = value * (points - nodes[other]) / (nodes[index] - nodes[other])
        columns.append(value)
    return jnp.stack(columns, axis=0)


def leaf(position, weight, phase):
    basis_x = lagrange(position[:, 0, :])
    basis_y = lagrange(position[:, 1, :])
    cosv = jnp.cos(phase)
    sinv = jnp.sin(phase)
    real = weight[:, 0, :] * cosv - weight[:, 1, :] * sinv
    imag = weight[:, 0, :] * sinv + weight[:, 1, :] * cosv
    part_re = jnp.einsum("akp,bkp->kab", basis_x * real, basis_y, precision=HIGH)
    part_im = jnp.einsum("akp,bkp->kab", basis_x * imag, basis_y, precision=HIGH)
    count = position.shape[0]
    return 0.5 * jnp.concatenate([part_re.reshape(count, 64), part_im.reshape(count, 64)], axis=1)


def translation(step, child):
    nodes = cheb_nodes()
    inner = lagrange((nodes + (2.0 * child - 1.0)) / 2.0).T
    eye_eight = jnp.eye(8, dtype=jnp.float32)
    if step % 2 == 0:
        middle = jnp.kron(inner, eye_eight)
    else:
        middle = jnp.kron(eye_eight, inner)
    return jnp.kron(jnp.eye(2, dtype=jnp.float32), middle)


def rotate(values, theta):
    cosv = jnp.cos(theta)
    sinv = jnp.sin(theta)
    real = values[..., :64]
    imag = values[..., 64:]
    return jnp.concatenate([cosv * real - sinv * imag, sinv * real + cosv * imag], axis=-1)


def level(own, partner, rate, bitval, step):
    theta = rate * (step + 1.0)
    own_t = rotate(own, theta)
    partner_t = rotate(partner, theta)
    first = jnp.where(bitval == 0, own_t, partner_t)
    second = jnp.where(bitval == 0, partner_t, own_t)
    left = jnp.einsum("...kt,tu->...ku", first, translation(step, 0), precision=HIGH)
    right = jnp.einsum("...kt,tu->...ku", second, translation(step, 1), precision=HIGH)
    return 0.70710678 * (left + right)


def evaluate(state, target_phase, side):
    grid = (2.0 * jnp.arange(side).astype(jnp.float32) + 1.0) / side - 1.0
    basis = lagrange(grid)
    table = jnp.einsum("am,bn->abmn", basis, basis, precision=HIGH).reshape(64, side * side)
    value_re = jnp.dot(state[:, :64], table, precision=HIGH)
    value_im = jnp.dot(state[:, 64:], table, precision=HIGH)
    cosv = jnp.cos(target_phase)
    sinv = jnp.sin(target_phase)
    return jnp.stack([value_re * cosv - value_im * sinv, value_re * sinv + value_im * cosv], axis=0)


def local(src_position, src_weight, src_phase, block_box, block_count, node_rate, target_phase):
    n_lo = lax.axis_size("lo")
    n_hi = lax.axis_size("hi")
    lo_index = lax.axis_index("lo")
    hi_index = lax.axis_index("hi")
    slots = block_box.shape[0]
    boxes = node_rate.shape[0]
    live = jnp.arange(slots) < block_count[0]
    coeff = jnp.where(live[:, None], leaf(src_position, src_weight, src_phase), 0.0)
    table = jax.ops.segment_sum(coeff, block_box, boxes * n_lo * n_hi)
    state = lax.psum_scatter(table, ("hi", "lo"), scatter_dimension=0, tiled=True)
    lo_bits = n_lo.bit_length() - 1
    hi_bits = n_hi.bit_length() - 1
    for bit in range(lo_bits):
        partner = partner_2(state, "lo", bit)
        bitval = lo_index >> bit & 1
        state = level(state, partner, node_rate, bitval, bit)
    for bit in range(hi_bits):
        partner = partner_2(state, "hi", bit)
        bitval = hi_index >> bit & 1
        state = level(state, partner, node_rate, bitval, lo_bits + bit)
    side = math.isqrt(target_phase.shape[1])
    return evaluate(state, target_phase, side)


def solution(mesh):
    placed = (
        P(("hi", "lo"), None, None),
        P(("hi", "lo"), None, None),
        P(("hi", "lo"), None),
        P(("hi", "lo")),
        P(("hi", "lo")),
        P(("hi", "lo"), None),
        P(("hi", "lo"), None),
    )
    return jax.shard_map(
        local, mesh=mesh, in_specs=placed, out_specs=P(None, ("hi", "lo"), None), check_vma=False
    )
```

profile of v0, /device:TPU:1, one launch (start us, length us, event | category | flops | bytes accessed | tf_op | source)
XLA Modules:
  0.0 927.6 jit_solution(14479246828985460735)
XLA Ops:
  6.6 0.7 fusion.97
  79.7 1.1 fusion.94
  80.8 4.6 bitcast_dynamic-update-slice_fusion.7
  85.4 4.6 multiply_divide_fusion.6
  90.0 4.6 multiply_divide_fusion.5
  94.6 4.6 bitcast_dynamic-update-slice_fusion.6
  99.2 4.5 multiply_divide_fusion.4
  103.7 4.5 bitcast_dynamic-update-slice_fusion.5
  108.3 4.5 multiply_divide_fusion.3
  112.8 4.5 bitcast_dynamic-update-slice_fusion.4
  117.4 4.6 multiply_divide_fusion.2
  122.0 4.6 bitcast_dynamic-update-slice_fusion.3
  126.6 4.6 multiply_divide_fusion.1
  131.2 4.6 bitcast_dynamic-update-slice_fusion.2
  135.8 4.5 multiply_divide_fusion
  140.4 4.5 bitcast_dynamic-update-slice_fusion.1
  144.9 4.6 multiply_divide_fusion.7
  149.5 4.6 bitcast_dynamic-update-slice_fusion
  154.2 1.1 fusion.93
  155.3 1.1 fusion.95
  156.5 0.8 stack.17
  157.3 1.2 fusion.11
  158.7 1.2 fusion.9
  160.9 7.9 scatter_custom_fusion
  168.8 17.4 %copy.57 = f32[32768,128]{0,1:T(8,128)} copy(f32[32768,128]{1,0:T(8,128)} %scatter_custom_fusion) | data formatting | bytes 33554432 | tf_op jit(solution)/shard_map/scatter-add | solution.py:97
  186.3 4.7 multiply_divide_fusion.8
  191.0 4.6 multiply_divide_fusion.9
  195.5 4.6 multiply_divide_fusion.10
  200.2 4.6 multiply_divide_fusion.11
  204.8 4.5 multiply_divide_fusion.12
  209.3 4.5 multiply_divide_fusion.13
  213.9 4.6 multiply_divide_fusion.14
  218.5 4.6 multiply_divide_fusion.15
  224.4 578.9 %reduce-scatter.2.cloned.1.call-done = f32[256,128]{0,1:T(8,128)} async-done(((f32[32768,128]{0,1:T(8,128)}), f32[256,128]{0,1:T(8,128)}) %reduce-scatter.2.cloned.1.call-update) | async-done | bytes 131088 | tf_op jit(solution)/shard_map/reduce_scatter | solution.py:98
  803.5 4.4 collective-permute-done
  807.9 0.9 multiply_subtract_fusion.13
  808.8 0.3 fusion.32
  809.2 0.3 fusion.2
  809.6 4.6 fusion.77
  814.4 4.5 fusion.76
  819.2 0.3 fusion.29
  820.0 4.6 fusion.75
  824.6 4.6 fusion.74
  829.4 0.3 fusion.26
  829.7 0.3 fusion.4
  830.2 4.5 fusion.73
  834.7 4.5 fusion.72
  839.5 0.3 fusion.23
  839.8 0.3 fusion.5
  840.2 4.5 fusion.71
  844.8 4.6 fusion.70
  849.7 0.3 fusion.20
  850.0 0.3 fusion.6
  850.3 57.9 %collective-permute-start.5 = (f32[256,128]{0,1:T(8,128)S(1)}, f32[256,128]{0,1:T(8,128)S(1)}, u32[]{:S(2)}, u32[]{:S(2)}) collective-permute-start(f32[256,128]{0,1:T(8,128)S(1)} %fusion.6), channel_id=1, source_target_pairs={{0,32},{32,0},{64,96},{96,64},{1,33},{33,1},{65,97},{97,65},{2,34}... | collective-permute-start | bytes 393224 | tf_op jit(solution)/shard_map/ppermute | solution.py:14
  908.6 0.6 collective-permute-done.5
  909.5 0.3 fusion.17
  909.8 0.3 fusion.7
  910.1 4.2 collective-permute-start.6
  914.4 0.9 fusion.92
  915.3 2.8 collective-permute-done.6
  918.7 0.3 fusion.8
  919.0 0.4 fusion.34
  919.5 0.4 subtract_bitcast_fusion
  919.9 0.8 pad_maximum_fusion
  (49 shorter events, 5.4 us)
Async XLA Ops:
  6.5 796.8 %reduce-scatter.2.cloned.1.call-start = ((), (), s32[]{:S(2)}) async-start(), calls=%async_computation.1 | async-start | bytes 16908288 | tf_op jit(solution)/shard_map/reduce_scatter | solution.py:98
  186.3 617.0 %copy-start = (f32[256,64]{0,1:T(8,128)S(1)}, f32[256,64]{0,1:T(8,128)}, u32[]{:S(2)}) copy-start(f32[256,64]{0,1:T(8,128)} %param.12) | copy-start | bytes 196612
  186.3 728.1 %copy-start.1 = (f32[256,256]{1,0:T(8,128)S(1)}, f32[256,256]{1,0:T(8,128)}, u32[]{:S(2)}) copy-start(f32[256,256]{1,0:T(8,128)} %param.13) | copy-start | bytes 786436
  803.3 4.6 collective-permute-start
  809.5 9.4 %collective-permute-start.1 = (f32[256,128]{0,1:T(8,128)S(1)}, f32[256,128]{0,1:T(8,128)S(1)}, u32[]{:S(2)}, u32[]{:S(2)}) collective-permute-start(f32[256,128]{0,1:T(8,128)S(1)} %fusion.2), channel_id=1, source_target_pairs={{0,2},{1,3},{2,0},{3,1},{4,6},{5,7},{6,4},{7,5},{8,10},{9,11},{10,... | collective-permute-start | bytes 393224 | tf_op jit(solution)/shard_map/ppermute | solution.py:14
  819.9 9.3 collective-permute-start.2
  830.1 9.1 collective-permute-start.3
  840.1 9.3 collective-permute-start.4
  850.3 58.9 %collective-permute-start.5 = (f32[256,128]{0,1:T(8,128)S(1)}, f32[256,128]{0,1:T(8,128)S(1)}, u32[]{:S(2)}, u32[]{:S(2)}) collective-permute-start(f32[256,128]{0,1:T(8,128)S(1)} %fusion.6), channel_id=1, source_target_pairs={{0,32},{32,0},{64,96},{96,64},{1,33},{33,1},{65,97},{97,65},{2,34}... | collective-permute-start | bytes 393224 | tf_op jit(solution)/shard_map/ppermute | solution.py:14
  910.1 8.0 collective-permute-start.6
Sparse Core Ops, SparseCore 0:
  186.4 616.8 reduce-scatter.1
where the time goes:
time: 933 us; the launch traced here: 928 us
  waiting for transfers between devices  587 us (63%)
  other arithmetic  158 us (17%)
  between operations  87 us (9%)
  starting transfers between devices  62.5 us (7%)
  local copies, waits for them, and re-layouts  25.3 us (3%)
    reduce_scatter x1, waiting for transfers between devices, local(): lax.psum_scatter(table, ('hi', 'lo'), scatter_dimension=0, tiled=True)  579 us
    div x24, other arithmetic, lagrange(): value = value * (points - nodes[other]) / (nodes[index] - nodes[other])  110 us
    ppermute x7, starting transfers between devices, partner_2(): return lax.ppermute(value, axis, pairs)  62.5 us
    unnamed x7, other arithmetic  32 us
  transfers between devices with their start and end apart: 8, of which 4 were waited for; matrix products, arithmetic and copies ran while one was open for 8% of the time, Pallas kernels for 0%

commit v1 on v0

v1 whole, which is shorter than its diff:
```python
import functools
import math

import jax
import jax.numpy as jnp
import ml_dtypes
import numpy as np
from jax import lax
from jax.experimental import pallas as pl
from jax.experimental.pallas import tpu as pltpu
from jax.sharding import PartitionSpec as P

MESH = pl.DeviceIdType.MESH
F32 = jnp.float32
BF16 = jnp.bfloat16
VMEM = pl.BlockSpec(memory_space=pltpu.VMEM)
SMEM = pl.BlockSpec(memory_space=pltpu.SMEM)
PAY = 136


def np_nodes():
    return np.cos((2.0 * np.arange(8) + 1.0) * math.pi / 16.0)


def np_lagrange(points):
    nodes = np_nodes()
    columns = []
    for index in range(8):
        value = np.ones_like(points)
        for other in range(8):
            if other != index:
                value = value * (points - nodes[other]) / (nodes[index] - nodes[other])
        columns.append(value)
    return np.stack(columns, axis=0)


def split_np(array):
    high = array.astype(np.float32).astype(ml_dtypes.bfloat16)
    low = (array - high.astype(np.float64)).astype(np.float32).astype(ml_dtypes.bfloat16)
    return high, low


def level_weight(parity):
    blocks = []
    for child in range(2):
        inner = np_lagrange((np_nodes() + (2.0 * child - 1.0)) / 2.0).T
        middle = np.kron(inner, np.eye(8)) if parity == 0 else np.kron(np.eye(8), inner)
        blocks.append(np.kron(np.eye(2), middle))
    weight = 0.70710678 * np.concatenate(blocks, axis=0)
    return np.concatenate(split_np(weight), axis=1)


def target_weight(side):
    grid = (2.0 * np.arange(side) + 1.0) / side - 1.0
    basis = np_lagrange(grid)
    table = np.einsum("am,bn->abmn", basis, basis).reshape(64, side * side)
    high, low = split_np(np.kron(np.eye(2), table))
    return np.concatenate([high, high, low], axis=0)


def sincos(angle):
    half = 0.5 * angle
    sq = half * half
    s = -1.0 / 39916800.0
    for term in (1.0 / 362880.0, -1.0 / 5040.0, 1.0 / 120.0, -1.0 / 6.0, 1.0):
        s = s * sq + term
    s = s * half
    c = 1.0 / 479001600.0
    for term in (-1.0 / 3628800.0, 1.0 / 40320.0, -1.0 / 720.0, 1.0 / 24.0, -0.5, 1.0):
        c = c * sq + term
    return 2.0 * s * c, 1.0 - 2.0 * s * s


def lagrange_rows(points):
    nodes = [float(v) for v in np_nodes()]
    diff = [points - v for v in nodes]
    before = [None] * 8
    after = [None] * 8
    for index in range(1, 8):
        before[index] = diff[0] if index == 1 else before[index - 1] * diff[index - 1]
    for index in range(6, -1, -1):
        after[index] = diff[7] if index == 6 else after[index + 1] * diff[index + 1]
    rows = []
    for index in range(8):
        scale = 1.0
        for other in range(8):
            if other != index:
                scale = scale / (nodes[index] - nodes[other])
        if index == 0:
            value = after[0]
        elif index == 7:
            value = before[7]
        else:
            value = before[index] * after[index]
        rows.append(value * scale)
    return rows


def split(value):
    high = value.astype(BF16)
    low = (value - high.astype(F32)).astype(BF16)
    return high, low


def leaf_kernel(pos_ref, wgt_ref, phase_ref, box_ref, count_ref, out_ref, gx, ly, ct):
    slots = phase_ref.shape[0]
    sinv, cosv = sincos(phase_ref[...])
    w_re = wgt_ref[pl.ds(0, slots, stride=2), :]
    w_im = wgt_ref[pl.ds(1, slots, stride=2), :]
    g_re = (0.5 * (w_re * cosv - w_im * sinv)).T
    g_im = (0.5 * (w_re * sinv + w_im * cosv)).T
    x = pos_ref[pl.ds(0, slots, stride=2), :].T
    y = pos_ref[pl.ds(1, slots, stride=2), :].T
    for index, value in enumerate(lagrange_rows(x)):
        gx[index] = value * g_re
        gx[8 + index] = value * g_im
    for index, value in enumerate(lagrange_rows(y)):
        ly[index] = value

    def row(index, carry):
        total = gx[index, 0:8, :][None] * ly[:, 0:8, :]
        for part in range(1, slots // 8):
            rows = slice(8 * part, 8 * part + 8)
            total = total + gx[index, rows, :][None] * ly[:, rows, :]
        ct[pl.ds(pl.multiple_of(index * 8, 8), 8), :] = jnp.sum(total, axis=1)
        return carry

    lax.fori_loop(0, 16, row, 0)
    out_ref[0:slots, :] = ct[...].T
    lane = lax.broadcasted_iota(jnp.int32, (1, slots), 1)
    key = jnp.where(lane < count_ref[0], box_ref[...], -1).astype(F32)
    out_ref[slots:slots + 8, :] = jnp.broadcast_to(key, (8, slots))


def butterfly_kernel(nxy, nq, pay_ref, rate_ref, w0_ref, w1_ref, out_ref,
                     gath, cat, rate_s, rate_r, rate_s2, rate_r2,
                     sib_s, sib_r, own, zrecv, ret_s, ret_r, fin_s, fin_r,
                     g_send, g_recv, r_send, r_recv, r2_send, r2_recv,
                     b_send, b_recv, z_send, z_recv, t_send, t_recv, f_send, f_recv):
    ndev = nxy * nq
    lb = 2 * ndev
    lx = nxy.bit_length() - 1
    slots = gath.shape[1] - 8
    hi = lax.axis_index("hi")
    lo = lax.axis_index("lo")
    xy = lax.div(lo, 2)
    zlo = lax.rem(lo, 2)
    q = hi * 2 + zlo
    core = lax.rem(hi, 2)
    z = lax.div(hi, 2) * 2 + zlo

    def dev(q_at, xy_at):
        return lax.div(q_at, 2), xy_at * 2 + lax.rem(q_at, 2)

    def xy_peer(step):
        return lax.rem(xy + step, nxy)

    def q_peer(step):
        return lax.rem(q + step, nq)

    def q_of(z_at, core_at):
        return lax.div(z_at, 2) * 4 + core_at * 2 + lax.rem(z_at, 2)

    def rcopy(src, dst, send, recv, target):
        return pltpu.make_async_remote_copy(
            src_ref=src, dst_ref=dst, send_sem=send, recv_sem=recv,
            device_id=target, device_id_type=MESH)

    barrier = pltpu.get_barrier_semaphore()

    def greet_xy(step, carry):
        pl.semaphore_signal(barrier, inc=1, device_id=dev(q, xy_peer(step)), device_id_type=MESH)
        return carry

    def greet_q(step, carry):
        pl.semaphore_signal(barrier, inc=1, device_id=dev(q_peer(step), xy), device_id_type=MESH)
        return carry

    lax.fori_loop(1, nxy, greet_xy, 0)
    lax.fori_loop(1, nq, greet_q, 0)

    rate_lo = rate_ref[0:ndev, :]
    rate_hi = rate_ref[ndev:lb, :]
    packed = jnp.concatenate([rate_lo, rate_hi], axis=1)
    rate_s[...] = packed.reshape(nxy, nq, 128)
    pl.semaphore_wait(barrier, nxy - 1 + nq - 1)

    def gather_copy(step):
        return rcopy(pay_ref, gath.at[xy], g_send.at[step], g_recv.at[step], dev(q, xy_peer(step)))

    def rate_copy(step):
        to = xy_peer(step)
        return rcopy(rate_s.at[to], rate_r.at[xy], r_send.at[step], r_recv.at[step], dev(q, to))

    def send_all(step, carry):
        gather_copy(step).start()
        return carry

    def send_rate(step, carry):
        rate_copy(step).start()
        return carry

    lax.fori_loop(1, nxy, send_rate, 0)
    lax.fori_loop(1, nxy, send_all, 0)
    gath[xy] = pay_ref[...]
    rate_r[xy] = rate_s[xy]

    def wait_rate(step, carry):
        rate_copy(step).wait()
        return carry

    lax.fori_loop(1, nxy, wait_rate, 0)
    turned = jnp.transpose(rate_r[...], (1, 0, 2))
    rate_s2[...] = turned

    def rate2_copy(step):
        to = q_peer(step)
        return rcopy(rate_s2.at[to], rate_r2.at[q], r2_send.at[step], r2_recv.at[step], dev(to, xy))

    def send_rate2(step, carry):
        rate2_copy(step).start()
        return carry

    lax.fori_loop(1, nq, send_rate2, 0)
    rate_r2[q] = rate_s2[q]

    def wait_gather(step, carry):
        gather_copy(step).wait()
        return carry

    lax.fori_loop(1, nxy, wait_gather, 0)

    def split_rows(index, carry):
        high, low = split(gath[index, 0:slots, :])
        rows = pl.ds(pl.multiple_of(index * slots, slots), slots)
        cat[rows, 0:128] = high
        cat[rows, 128:256] = low
        return carry

    lax.fori_loop(0, nxy, split_rows, 0)

    n = gath[:, slots, :].astype(jnp.int32)
    lbits = lb.bit_length() - 1
    dbits = ndev.bit_length() - 1
    j = n & (lb - 1)
    owner = n >> lbits
    holder = j & (ndev - 1)
    q_d = ((owner >> (lx + 1)) << 1) | (owner & 1)
    xy_d = (owner >> 1) & (nxy - 1)
    local = ((j >> dbits) << dbits) + q_d * nxy + xy_d
    code = (holder & (nq - 1)) * lb + local
    code = jnp.where((n >= 0) & ((holder >> 3) == xy), code, -1)
    row_id = lax.broadcasted_iota(jnp.int32, (lb, slots), 0)

    def chunk(q_at):
        rel = code - q_at * lb
        hot = [jnp.where(rel[i:i + 1, :] == row_id, 1.0, 0.0).astype(BF16) for i in range(nxy)]
        both = jnp.dot(jnp.concatenate(hot, axis=1), cat[...], preferred_element_type=F32)
        return both[:, 0:128] + both[:, 128:256]

    def sib_copy(off):
        return rcopy(sib_s.at[off], sib_r.at[off], b_send.at[off], b_recv.at[off],
                     dev(q_of(z, 1 - core), xy))

    def z_copy(off):
        return rcopy(own.at[off], zrecv.at[off], z_send.at[off], z_recv.at[off],
                     dev(q_of(lax.rem(z + off, 4), core), xy))

    def fold(off):
        sib_copy(off).wait()
        own[off] = own[off] + sib_r[off]

    def scatter(step, carry):
        off = 3 - step
        to = lax.rem(z + off, 4)
        sib_s[off] = chunk(q_of(to, 1 - core))
        sib_copy(off).start()

        @pl.when(step >= 1)
        def _():
            fold(off + 1)
            z_copy(off + 1).start()

        own[off] = chunk(q_of(to, core))
        return carry

    lax.fori_loop(0, 4, scatter, 0)

    def wait_rate2(step, carry):
        rate2_copy(step).wait()
        return carry

    lax.fori_loop(1, nq, wait_rate2, 0)
    sin_p, cos_p = sincos(rate_r2[...].reshape(ndev, 128))
    left = lax.broadcasted_iota(jnp.int32, (ndev, 128), 1) < 64
    cos_o = pltpu.roll(cos_p, 64, 1)
    sin_o = pltpu.roll(sin_p, 64, 1)
    cos1 = jnp.concatenate([jnp.where(left, cos_p, cos_o), jnp.where(left, cos_o, cos_p)], axis=0)
    sin1 = jnp.concatenate([jnp.where(left, -sin_p, sin_o), jnp.where(left, -sin_o, sin_p)], axis=0)

    fold(0)

    def wait_z(step, carry):
        z_copy(step).wait()
        own[0] = own[0] + zrecv[step]
        return carry

    lax.fori_loop(1, 4, wait_z, 0)

    state = own[0]
    cosv, sinv = cos1, sin1
    sub = lax.broadcasted_iota(jnp.int32, (lb // 8, 8, 128), 1)
    for step in range(dbits):
        if step > 0:
            cosv, sinv = cosv * cos1 - sinv * sin1, sinv * cos1 + cosv * sin1
        bit = lx if step == 0 else (step - 1 if step <= lx else step)
        if bit < 3:
            tiles = state.reshape(lb // 8, 8, 128)
            dist = 1 << bit
            upper = (sub & dist) != 0
            first = jnp.where(upper, pltpu.roll(tiles, dist, 1), tiles).reshape(lb, 128)
            second = jnp.where(upper, tiles, pltpu.roll(tiles, 8 - dist, 1)).reshape(lb, 128)
        else:
            pairs = state.reshape(lb >> (bit + 1), 2, 1 << bit, 128)
            first = jnp.concatenate([pairs[:, 0:1], pairs[:, 0:1]], axis=1).reshape(lb, 128)
            second = jnp.concatenate([pairs[:, 1:2], pairs[:, 1:2]], axis=1).reshape(lb, 128)
        first = cosv * first + sinv * pltpu.roll(first, 64, 1)
        second = cosv * second + sinv * pltpu.roll(second, 64, 1)
        high, low = split(jnp.concatenate([first, second], axis=1))
        w_ref = w0_ref if step % 2 == 0 else w1_ref
        main = jnp.dot(high, w_ref[...], preferred_element_type=F32)
        rest = jnp.dot(low, w_ref[:, 0:128], preferred_element_type=F32)
        state = main[:, 0:128] + (main[:, 128:256] + rest)

    for jj in range(2):
        ret_s[:, jj] = state[jj * ndev:(jj + 1) * ndev].reshape(nq, nxy, 128)

    def ret_copy(step):
        to = q_peer(step)
        return rcopy(ret_s.at[to], ret_r.at[q], t_send.at[step], t_recv.at[step], dev(to, xy))

    def send_ret(step, carry):
        ret_copy(step).start()
        return carry

    def wait_ret(step, carry):
        ret_copy(step).wait()
        return carry

    lax.fori_loop(1, nq, send_ret, 0)
    ret_r[q] = ret_s[q]
    lax.fori_loop(1, nq, wait_ret, 0)
    back = ret_r[...].reshape(nq * 2, nxy, 128)
    fin_s[...] = jnp.transpose(back, (1, 0, 2))

    def fin_copy(step):
        to = xy_peer(step)
        return rcopy(fin_s.at[to], fin_r.at[xy], f_send.at[step], f_recv.at[step], dev(q, to))

    def send_fin(step, carry):
        fin_copy(step).start()
        return carry

    def wait_fin(step, carry):
        fin_copy(step).wait()
        return carry

    lax.fori_loop(1, nxy, send_fin, 0)
    fin_r[xy] = fin_s[xy]
    lax.fori_loop(1, nxy, wait_fin, 0)
    out_ref[...] = fin_r[...].reshape(lb, 128)


def target_kernel(state_ref, phase_ref, table_ref, out_ref):
    lb, points = phase_ref.shape
    half = lb // 2
    for jj in range(2):
        rows = slice(jj * half, jj * half + half)
        high, low = split(state_ref[pl.ds(jj, half, stride=2), :])
        stacked = jnp.concatenate([high, low, high], axis=1)
        value = jnp.dot(stacked, table_ref[...], preferred_element_type=F32)
        sinv, cosv = sincos(phase_ref[rows, :])
        v_re = value[:, 0:points]
        v_im = value[:, points:2 * points]
        out_ref[0, rows, :] = v_re * cosv - v_im * sinv
        out_ref[1, rows, :] = v_re * sinv + v_im * cosv


def local(nxy, nq, side, src_position, src_weight, src_phase, block_box, block_count, node_rate, target_phase):
    slots, points = src_phase.shape
    lb = node_rate.shape[0]
    ndev = nxy * nq
    payload = pl.pallas_call(
        leaf_kernel,
        out_shape=jax.ShapeDtypeStruct((slots + 8, 128), F32),
        in_specs=[VMEM, VMEM, VMEM, VMEM, SMEM],
        out_specs=VMEM,
        scratch_shapes=[
            pltpu.VMEM((16, points, slots), F32),
            pltpu.VMEM((8, points, slots), F32),
            pltpu.VMEM((128, slots), F32),
        ],
        compiler_params=pltpu.CompilerParams(vmem_limit_bytes=32 * 2**20),
        name="leaf",
    )(src_position.reshape(2 * slots, points), src_weight.reshape(2 * slots, points), src_phase,
      block_box.reshape(1, slots), block_count)

    dma = pltpu.SemaphoreType.DMA
    state = pl.pallas_call(
        functools.partial(butterfly_kernel, nxy, nq),
        out_shape=jax.ShapeDtypeStruct((lb, 128), F32),
        in_specs=[VMEM] * 4,
        out_specs=VMEM,
        scratch_shapes=[
            pltpu.VMEM((nxy, slots + 8, 128), F32),
            pltpu.VMEM((nxy * slots, 256), BF16),
            pltpu.VMEM((nxy, nq, 128), F32),
            pltpu.VMEM((nxy, nq, 128), F32),
            pltpu.VMEM((nq, nxy, 128), F32),
            pltpu.VMEM((nq, nxy, 128), F32),
            pltpu.VMEM((4, lb, 128), F32),
            pltpu.VMEM((4, lb, 128), F32),
            pltpu.VMEM((4, lb, 128), F32),
            pltpu.VMEM((4, lb, 128), F32),
            pltpu.VMEM((nq, 2, nxy, 128), F32),
            pltpu.VMEM((nq, 2, nxy, 128), F32),
            pltpu.VMEM((nxy, 2 * nq, 128), F32),
            pltpu.VMEM((nxy, 2 * nq, 128), F32),
            dma((nxy,)), dma((nxy,)), dma((nxy,)), dma((nxy,)), dma((nq,)), dma((nq,)),
            dma((4,)), dma((4,)), dma((4,)), dma((4,)),
            dma((nq,)), dma((nq,)), dma((nxy,)), dma((nxy,)),
        ],
        compiler_params=pltpu.CompilerParams(
            collective_id=0, has_side_effects=True, vmem_limit_bytes=48 * 2**20),
        name="butterfly",
    )(payload, node_rate, level_weight(0), level_weight(1))

    return pl.pallas_call(
        target_kernel,
        out_shape=jax.ShapeDtypeStruct((2, lb, target_phase.shape[1]), F32),
        in_specs=[VMEM] * 3,
        out_specs=VMEM,
        compiler_params=pltpu.CompilerParams(vmem_limit_bytes=32 * 2**20),
        name="target",
    )(state, target_phase, target_weight(side))


def solution(mesh):
    n_hi, n_lo = mesh.shape["hi"], mesh.shape["lo"]
    placed = (
        P(("hi", "lo"), None, None),
        P(("hi", "lo"), None, None),
        P(("hi", "lo"), None),
        P(("hi", "lo")),
        P(("hi", "lo")),
        P(("hi", "lo"), None),
        P(("hi", "lo"), None),
    )
    return jax.shard_map(
        functools.partial(local, n_lo // 2, 2 * n_hi, 16),
        mesh=mesh, in_specs=placed, out_specs=P(None, ("hi", "lo"), None), check_vma=False
    )
```

time: 933 us -> 55.5 us (0.06)
  waiting for transfers between devices: 587 us -> 0 us
  other arithmetic: 158 us -> 0 us
  between operations: 87 us -> 0.74 us
  starting transfers between devices: 62.5 us -> 0 us
  Pallas kernels: 0 us -> 51.1 us
  local copies, waits for them, and re-layouts: 25.3 us -> 3.41 us
    reduce_scatter x1 -> x0, waiting for transfers between devices: 579 us -> none  [local(): lax.psum_scatter(table, ('hi', 'lo'), scatter_dimension=0, tiled=True)]
    div x24 -> x0, other arithmetic: 110 us -> none  [lagrange(): value = value * (points - nodes[other]) / (nodes[index] - nodes[other])]
    ppermute x7 -> x0, starting transfers between devices: 62.5 us -> none  [partner_2(): return lax.ppermute(value, axis, pairs)]
    pallas_call x0 -> x3, Pallas kernels: none -> 51.1 us  [the longest x1 48.7 us: local(): pl.pallas_call(functools.partial(butterfly_kernel, nxy, nq), out_shape=ja...]
    unnamed x7 -> x0, other arithmetic: 32 us -> none
    scatter-add x1 -> x0, local copies, waits for them, and re-layouts: 17.4 us -> none  [local(): table = jax.ops.segment_sum(coeff, block_box, boxes * n_lo * n_hi)]
  transfers between devices with their start and end apart: 8 -> 0, of which waited for: 4 -> 0; matrix products, arithmetic and copies ran while one was open for 8% -> 0% of each run, Pallas kernels for 0% -> 0%
where the time goes in v1:
time: 55.5 us; the launch traced here: 55.3 us
  Pallas kernels  51.1 us (92%)
  local copies, waits for them, and re-layouts  3.41 us (6%)
  between operations  0.74 us (1%)
    pallas_call x1, Pallas kernels, local(): pl.pallas_call(functools.partial(butterfly_kernel, nxy, nq), out_shape=ja...  48.7 us
    unnamed x19, local copies, waits for them, and re-layouts  3.41 us
    pallas_call x1, Pallas kernels, local(): pl.pallas_call(leaf_kernel, out_shape=jax.ShapeDtypeStruct((slots + 8, 12...  1.25 us
    pallas_call x1, Pallas kernels, local(): pl.pallas_call(target_kernel, out_shape=jax.ShapeDtypeStruct((2, lb, targ...  1.23 us

profile of v1, /device:TPU:1, one launch (start us, length us, event | category | flops | bytes accessed | tf_op | source)
XLA Modules:
  0.0 55.3 jit_solution(842909327207460048)
XLA Ops:
  0.7 0.0 copy-start.7
  0.7 0.6 %copy-done.7 = s32[128]{0:T(128)S(1)} copy-done((s32[128]{0:T(128)S(1)}, s32[128]{0:T(128)}, u32[]{:S(2)}) %copy-start.7) | copy-done | bytes 536
  1.3 0.0 copy-start.2
  1.3 0.9 %copy-done.2 = f32[128,2,128]{2,1,0:T(2,128)S(1)} copy-done((f32[128,2,128]{2,1,0:T(2,128)S(1)}, f32[128,2,128]{2,1,0:T(2,128)}, u32[]{:S(2)}) %copy-start.2) | copy-done | bytes 131096
  2.2 0.0 copy-start.3
  2.2 0.9 %copy-done.3 = f32[128,2,128]{2,1,0:T(2,128)S(1)} copy-done((f32[128,2,128]{2,1,0:T(2,128)S(1)}, f32[128,2,128]{2,1,0:T(2,128)}, u32[]{:S(2)}) %copy-start.3) | copy-done | bytes 131096
  3.1 0.0 copy-start.6
  3.1 0.8 %copy-done.6 = f32[128,128]{1,0:T(8,128)S(1)} copy-done((f32[128,128]{1,0:T(8,128)S(1)}, f32[128,128]{1,0:T(8,128)}, u32[]{:S(2)}) %copy-start.6) | copy-done | bytes 65560
  4.0 0.0 copy-start.8
  4.0 0.0 copy-start.4
  4.0 0.0 copy-start.5
  4.0 1.2 %leaf.1.pay_ref = f32[136,128]{1,0:T(8,128)S(1)} custom-call(f32[256,128]{1,0:T(8,128)S(1)} %bitcast.3, f32[256,128]{1,0:T(8,128)S(1)} %bitcast.4, f32[128,128]{1,0:T(8,128)S(1)} %copy-done.6, s32[1,128]{1,0:T(1,128)S(1)} %bitcast.5, s32[1]{0:T(128)S(6)} %copy.12.count_ref), custom_call_target="tpu_custom_call" | custom-call | tf_op jit(solution)/shard_map/leaf/pallas_call | solution.py:393
  5.2 0.0 copy-done.8
  5.2 0.0 copy-start
  5.2 0.1 copy.11.rate_ref
  5.3 0.0 copy-done.4
  5.3 0.0 copy-done.5
  5.4 0.0 copy-start.1
  5.4 48.7 %butterfly.1.state_ref = f32[256,128]{1,0:T(8,128)S(1)} custom-call(f32[136,128]{1,0:T(8,128)S(1)} %leaf.1.pay_ref, f32[256,64]{1,0:T(8,128)S(1)} %copy.11.rate_ref, bf16[256,256]{1,0:T(8,128)(2,1)S(1)} %copy-done.5, bf16[256,256]{1,0:T(8,128)(2,1)S(1)} %copy-done.4), custom_call_target="tpu_custom_call" | custom-call | tf_op jit(solution)/shard_map/butterfly/pallas_call | solution.py:409
  54.0 0.0 copy-done
  54.0 0.0 copy-done.1
  54.1 1.2 %target.1 = f32[2,256,256]{2,1,0:T(8,128)} custom-call(f32[256,128]{1,0:T(8,128)S(1)} %butterfly.1.state_ref, f32[256,256]{1,0:T(8,128)S(1)} %copy-done.1, bf16[384,512]{1,0:T(8,128)(2,1)S(1)} %copy-done), custom_call_target="tpu_custom_call" | custom-call | tf_op jit(solution)/shard_map/target/pallas_call | solution.py:438
Async XLA Ops:
  0.7 0.7 %copy-start.7 = (s32[128]{0:T(128)S(1)}, s32[128]{0:T(128)}, u32[]{:S(2)}) copy-start(s32[128]{0:T(128)} %param.13) | copy-start | bytes 1540
  1.3 0.9 %copy-start.2 = (f32[128,2,128]{2,1,0:T(2,128)S(1)}, f32[128,2,128]{2,1,0:T(2,128)}, u32[]{:S(2)}) copy-start(f32[128,2,128]{2,1,0:T(2,128)} %param.10) | copy-start | bytes 393220
  2.2 0.9 %copy-start.3 = (f32[128,2,128]{2,1,0:T(2,128)S(1)}, f32[128,2,128]{2,1,0:T(2,128)}, u32[]{:S(2)}) copy-start(f32[128,2,128]{2,1,0:T(2,128)} %param.11) | copy-start | bytes 393220
  3.1 0.8 %copy-start.6 = (f32[128,128]{1,0:T(8,128)S(1)}, f32[128,128]{1,0:T(8,128)}, u32[]{:S(2)}) copy-start(f32[128,128]{1,0:T(8,128)} %phase_ref.2) | copy-start | bytes 196612
  4.0 1.3 %copy-start.8 = (f32[256,64]{0,1:T(8,128)S(1)}, f32[256,64]{0,1:T(8,128)}, u32[]{:S(2)}) copy-start(f32[256,64]{0,1:T(8,128)} %param.15) | copy-start | bytes 196612
  4.0 1.4 %copy-start.4 = (bf16[256,256]{1,0:T(8,128)(2,1)S(1)}, bf16[256,256]{1,0:T(8,128)(2,1)}, u32[]{:S(2)}) copy-start(bf16[256,256]{1,0:T(8,128)(2,1)} %constant.7.clone.w1_ref) | copy-start | bytes 393220
  4.0 1.4 %copy-start.5 = (bf16[256,256]{1,0:T(8,128)(2,1)S(1)}, bf16[256,256]{1,0:T(8,128)(2,1)}, u32[]{:S(2)}) copy-start(bf16[256,256]{1,0:T(8,128)(2,1)} %constant.6.clone.w0_ref) | copy-start | bytes 393220
  5.2 48.8 %copy-start = (bf16[384,512]{1,0:T(8,128)(2,1)S(1)}, bf16[384,512]{1,0:T(8,128)(2,1)}, u32[]{:S(2)}) copy-start(bf16[384,512]{1,0:T(8,128)(2,1)} %constant.8.clone.table_ref) | copy-start | bytes 1179652
  5.4 48.7 %copy-start.1 = (f32[256,256]{1,0:T(8,128)S(1)}, f32[256,256]{1,0:T(8,128)}, u32[]{:S(2)}) copy-start(f32[256,256]{1,0:T(8,128)} %phase_ref.3) | copy-start | bytes 786436

commit v2 on v1

--- a/solution.py
+++ b/solution.py
@@ -15,7 +15,6 @@
 BF16 = jnp.bfloat16
 VMEM = pl.BlockSpec(memory_space=pltpu.VMEM)
 SMEM = pl.BlockSpec(memory_space=pltpu.SMEM)
-PAY = 136
 
 
 def np_nodes():
@@ -102,7 +101,7 @@
     return high, low
 
 
-def leaf_kernel(pos_ref, wgt_ref, phase_ref, box_ref, count_ref, out_ref, gx, ly, ct):
+def leaf(pos_ref, wgt_ref, phase_ref, gx, ly, ct):
     slots = phase_ref.shape[0]
     sinv, cosv = sincos(phase_ref[...])
     w_re = wgt_ref[pl.ds(0, slots, stride=2), :]
@@ -126,21 +125,20 @@
         return carry
 
     lax.fori_loop(0, 16, row, 0)
-    out_ref[0:slots, :] = ct[...].T
-    lane = lax.broadcasted_iota(jnp.int32, (1, slots), 1)
-    key = jnp.where(lane < count_ref[0], box_ref[...], -1).astype(F32)
-    out_ref[slots:slots + 8, :] = jnp.broadcast_to(key, (8, slots))
-
-
-def butterfly_kernel(nxy, nq, pay_ref, rate_ref, w0_ref, w1_ref, out_ref,
-                     gath, cat, rate_s, rate_r, rate_s2, rate_r2,
-                     sib_s, sib_r, own, zrecv, ret_s, ret_r, fin_s, fin_r,
-                     g_send, g_recv, r_send, r_recv, r2_send, r2_recv,
+    return ct[...].T
+
+
+def butterfly_kernel(pos_hbm, wgt_hbm, phase_hbm, rate_hbm, w0_hbm, w1_hbm, box_ref, count_ref, out_ref,
+                     pos_ref, wgt_ref, phase_ref, rate_ref, w0_ref, w1_ref, gx, ly, ct,
+                     gath_a, gath_b, cat, rate_s, rate_r, rate_s2, rate_r2,
+                     sib_s, sib_r, own, zrecv, z2recv, ret_s, ret_r, fin_s, fin_r,
+                     in_sem, g_send, g_recv, r_send, r_recv, r2_send, r2_recv,
                      b_send, b_recv, z_send, z_recv, t_send, t_recv, f_send, f_recv):
+    nxy, nq = 16, 8
     ndev = nxy * nq
     lb = 2 * ndev
-    lx = nxy.bit_length() - 1
-    slots = gath.shape[1] - 8
+    lx = 4
+    slots = 128
     hi = lax.axis_index("hi")
     lo = lax.axis_index("lo")
     xy = lax.div(lo, 2)
@@ -149,6 +147,15 @@
     core = lax.rem(hi, 2)
     z = lax.div(hi, 2) * 2 + zlo
 
+    loads = [
+        pltpu.make_async_copy(src, dst, in_sem.at[i])
+        for i, (src, dst) in enumerate([
+            (phase_hbm, phase_ref), (wgt_hbm, wgt_ref), (pos_hbm, pos_ref),
+            (rate_hbm, rate_ref), (w0_hbm, w0_ref), (w1_hbm, w1_ref)])
+    ]
+    for load in loads:
+        load.start()
+
     def dev(q_at, xy_at):
         return lax.div(q_at, 2), xy_at * 2 + lax.rem(q_at, 2)
 
@@ -179,39 +186,95 @@
     lax.fori_loop(1, nxy, greet_xy, 0)
     lax.fori_loop(1, nq, greet_q, 0)
 
-    rate_lo = rate_ref[0:ndev, :]
-    rate_hi = rate_ref[ndev:lb, :]
-    packed = jnp.concatenate([rate_lo, rate_hi], axis=1)
-    rate_s[...] = packed.reshape(nxy, nq, 128)
+    x_at = lax.rem(xy, 4)
+    y_at = lax.div(xy, 4)
+    for load in loads[0:3]:
+        load.wait()
+    coeff = leaf(pos_ref, wgt_ref, phase_ref, gx, ly, ct)
+    lane = lax.broadcasted_iota(jnp.int32, (1, slots), 1)
+    key = jnp.where(lane < count_ref[0], box_ref[...], -1).astype(F32)
+    gath_a[y_at * 4 + x_at, 0:64, :] = coeff[64:128]
+    gath_a[y_at * 4 + x_at, 64:72, :] = jnp.broadcast_to(key, (8, slots))
+    gath_b[x_at * 4 + y_at] = coeff[0:64]
+    loads[3].wait()
+    rate_s[...] = jnp.concatenate([rate_ref[:, 0:ndev], rate_ref[:, ndev:lb]], axis=0).T
     pl.semaphore_wait(barrier, nxy - 1 + nq - 1)
 
-    def gather_copy(step):
-        return rcopy(pay_ref, gath.at[xy], g_send.at[step], g_recv.at[step], dev(q, xy_peer(step)))
+    xs = {0: x_at, -1: lax.rem(x_at + 3, 4), 1: lax.rem(x_at + 1, 4), 2: lax.rem(x_at + 2, 4)}
+    ys = {0: y_at, -1: lax.rem(y_at + 3, 4), 1: lax.rem(y_at + 1, 4), 2: lax.rem(y_at + 2, 4)}
+    order = (0, -1, 1, 2)
+    sent = []
+
+    def block(part, first, second, rows=None):
+        ref = gath_a if part == 0 else gath_b
+        at = ys[second] * 4 + xs[first] if part == 0 else xs[second] * 4 + ys[first]
+        return ref.at[at] if rows is None else ref.at[at, rows]
+
+    def halves(part):
+        return (slice(0, 40), slice(40, 72)) if part == 0 else (slice(0, 32), slice(32, 64))
+
+    def ring_copy(part, axis, sem, first, second, way, rows=None):
+        along_x = (part == 0) == (axis == 0)
+        to = ys[0] * 4 + xs[way] if along_x else ys[way] * 4 + xs[0]
+        ref = block(part, first, second, rows)
+        return rcopy(ref, ref, g_send.at[part, sem], g_recv.at[part, sem], dev(q, to))
+
+    def start(copy):
+        copy.start()
+        sent.append(copy)
+
+    for part in range(2):
+        start(ring_copy(part, 0, 0, 0, 0, 1))
+        start(ring_copy(part, 0, 1, 0, 0, -1))
+    for part in range(2):
+        start(ring_copy(part, 1, 4, 0, 0, 1))
+        start(ring_copy(part, 1, 5, 0, 0, -1))
 
     def rate_copy(step):
         to = xy_peer(step)
-        return rcopy(rate_s.at[to], rate_r.at[xy], r_send.at[step], r_recv.at[step], dev(q, to))
-
-    def send_all(step, carry):
-        gather_copy(step).start()
-        return carry
+        rows_to = pl.ds(pl.multiple_of(to * nq, nq), nq)
+        rows_me = pl.ds(pl.multiple_of(xy * nq, nq), nq)
+        return rcopy(rate_s.at[rows_to], rate_r.at[rows_me], r_send.at[step], r_recv.at[step], dev(q, to))
 
     def send_rate(step, carry):
         rate_copy(step).start()
         return carry
 
     lax.fori_loop(1, nxy, send_rate, 0)
-    lax.fori_loop(1, nxy, send_all, 0)
-    gath[xy] = pay_ref[...]
-    rate_r[xy] = rate_s[xy]
+    rows_me = pl.ds(pl.multiple_of(xy * nq, nq), nq)
+    rate_r[rows_me, :] = rate_s[rows_me, :]
+
+    for part in range(2):
+        low, high = halves(part)
+        ring_copy(part, 0, 0, -1, 0, 1).wait_recv()
+        start(ring_copy(part, 0, 2, -1, 0, 1, low))
+        ring_copy(part, 0, 1, 1, 0, -1).wait_recv()
+        start(ring_copy(part, 0, 3, 1, 0, -1, high))
+    for part in range(2):
+        for r in (1, 2):
+            start(ring_copy(part, 1, 4 + 4 * r, order[r], 0, 1))
+            start(ring_copy(part, 1, 5 + 4 * r, order[r], 0, -1))
+    for part in range(2):
+        low, high = halves(part)
+        ring_copy(part, 0, 2, 2, 0, 1, low).wait_recv()
+        ring_copy(part, 0, 3, 2, 0, -1, high).wait_recv()
+        start(ring_copy(part, 1, 4 + 12, 2, 0, 1))
+        start(ring_copy(part, 1, 5 + 12, 2, 0, -1))
+    for r in range(4):
+        for part in range(2):
+            low, high = halves(part)
+            ring_copy(part, 1, 4 + 4 * r, order[r], -1, 1).wait_recv()
+            start(ring_copy(part, 1, 6 + 4 * r, order[r], -1, 1, low))
+            ring_copy(part, 1, 5 + 4 * r, order[r], 1, -1).wait_recv()
+            start(ring_copy(part, 1, 7 + 4 * r, order[r], 1, -1, high))
 
     def wait_rate(step, carry):
         rate_copy(step).wait()
         return carry
 
     lax.fori_loop(1, nxy, wait_rate, 0)
-    turned = jnp.transpose(rate_r[...], (1, 0, 2))
-    rate_s2[...] = turned
+    for at in range(nq):
+        rate_s2[at] = rate_r[pl.ds(at, nxy, stride=nq), :]
 
     def rate2_copy(step):
         to = q_peer(step)
@@ -224,22 +287,26 @@
     lax.fori_loop(1, nq, send_rate2, 0)
     rate_r2[q] = rate_s2[q]
 
-    def wait_gather(step, carry):
-        gather_copy(step).wait()
-        return carry
-
-    lax.fori_loop(1, nxy, wait_gather, 0)
+    for r in range(4):
+        for part in range(2):
+            low, high = halves(part)
+            ring_copy(part, 1, 6 + 4 * r, order[r], 2, 1, low).wait_recv()
+            ring_copy(part, 1, 7 + 4 * r, order[r], 2, -1, high).wait_recv()
 
     def split_rows(index, carry):
-        high, low = split(gath[index, 0:slots, :])
-        rows = pl.ds(pl.multiple_of(index * slots, slots), slots)
-        cat[rows, 0:128] = high
-        cat[rows, 128:256] = low
+        rows_a = pl.ds(pl.multiple_of(index * slots + 64, 64), 64)
+        rows_b = pl.ds(pl.multiple_of(index * slots, 64), 64)
+        high, low = split(gath_a[index, 0:64, :])
+        cat[rows_a, 0:128] = high
+        cat[rows_a, 128:256] = low
+        high, low = split(gath_b[lax.rem(index, 4) * 4 + lax.div(index, 4)])
+        cat[rows_b, 0:128] = high
+        cat[rows_b, 128:256] = low
         return carry
 
     lax.fori_loop(0, nxy, split_rows, 0)
 
-    n = gath[:, slots, :].astype(jnp.int32)
+    n = gath_a[:, 64, :].astype(jnp.int32)
     lbits = lb.bit_length() - 1
     dbits = ndev.bit_length() - 1
     j = n & (lb - 1)
@@ -247,8 +314,8 @@
     holder = j & (ndev - 1)
     q_d = ((owner >> (lx + 1)) << 1) | (owner & 1)
     xy_d = (owner >> 1) & (nxy - 1)
-    local = ((j >> dbits) << dbits) + q_d * nxy + xy_d
-    code = (holder & (nq - 1)) * lb + local
+    local_row = ((j >> dbits) << dbits) + q_d * nxy + xy_d
+    code = (holder & (nq - 1)) * lb + local_row
     code = jnp.where((n >= 0) & ((holder >> 3) == xy), code, -1)
     row_id = lax.broadcasted_iota(jnp.int32, (lb, slots), 0)
 
@@ -262,29 +329,46 @@
         return rcopy(sib_s.at[off], sib_r.at[off], b_send.at[off], b_recv.at[off],
                      dev(q_of(z, 1 - core), xy))
 
-    def z_copy(off):
-        return rcopy(own.at[off], zrecv.at[off], z_send.at[off], z_recv.at[off],
-                     dev(q_of(lax.rem(z + off, 4), core), xy))
+    def z_dev(off):
+        return dev(q_of(lax.rem(z + off, 4), core), xy)
+
+    up_half = rcopy(own.at[2, 0:ndev], z2recv.at[0], z_send.at[0], z_recv.at[0], z_dev(1))
+    down_half = rcopy(own.at[2, ndev:lb], z2recv.at[1], z_send.at[1], z_recv.at[1], z_dev(3))
+    up_full = rcopy(own.at[1], zrecv.at[0], z_send.at[2], z_recv.at[2], z_dev(1))
+    down_full = rcopy(own.at[3], zrecv.at[1], z_send.at[3], z_recv.at[3], z_dev(3))
 
     def fold(off):
         sib_copy(off).wait()
         own[off] = own[off] + sib_r[off]
 
     def scatter(step, carry):
-        off = 3 - step
+        off = lax.rem(step + 2, 4)
         to = lax.rem(z + off, 4)
         sib_s[off] = chunk(q_of(to, 1 - core))
         sib_copy(off).start()
 
-        @pl.when(step >= 1)
+        @pl.when(step == 1)
         def _():
-            fold(off + 1)
-            z_copy(off + 1).start()
+            fold(2)
+            up_half.start()
+            down_half.start()
+
+        @pl.when(step == 3)
+        def _():
+            fold(3)
+            down_half.wait_recv()
+            own[3, ndev:lb] = own[3, ndev:lb] + z2recv[1]
+            down_full.start()
 
         own[off] = chunk(q_of(to, core))
         return carry
 
     lax.fori_loop(0, 4, scatter, 0)
+    fold(1)
+    up_half.wait_recv()
+    own[1, 0:ndev] = own[1, 0:ndev] + z2recv[0]
+    up_full.start()
+    fold(0)
 
     def wait_rate2(step, carry):
         rate2_copy(step).wait()
@@ -297,17 +381,13 @@
     sin_o = pltpu.roll(sin_p, 64, 1)
     cos1 = jnp.concatenate([jnp.where(left, cos_p, cos_o), jnp.where(left, cos_o, cos_p)], axis=0)
     sin1 = jnp.concatenate([jnp.where(left, -sin_p, sin_o), jnp.where(left, -sin_o, sin_p)], axis=0)
-
-    fold(0)
-
-    def wait_z(step, carry):
-        z_copy(step).wait()
-        own[0] = own[0] + zrecv[step]
-        return carry
-
-    lax.fori_loop(1, 4, wait_z, 0)
-
-    state = own[0]
+    for load in loads[4:6]:
+        load.wait()
+
+    down_full.wait_recv()
+    up_full.wait_recv()
+    state = own[0] + (zrecv[0] + zrecv[1])
+
     cosv, sinv = cos1, sin1
     sub = lax.broadcasted_iota(jnp.int32, (lb // 8, 8, 128), 1)
     for step in range(dbits):
@@ -332,12 +412,15 @@
         rest = jnp.dot(low, w_ref[:, 0:128], preferred_element_type=F32)
         state = main[:, 0:128] + (main[:, 128:256] + rest)
 
-    for jj in range(2):
-        ret_s[:, jj] = state[jj * ndev:(jj + 1) * ndev].reshape(nq, nxy, 128)
+    for at in range(nq):
+        for jj in range(2):
+            base = jj * ndev + at * nxy
+            ret_s[at, jj * nxy:(jj + 1) * nxy] = state[base:base + nxy]
 
     def ret_copy(step):
         to = q_peer(step)
-        return rcopy(ret_s.at[to], ret_r.at[q], t_send.at[step], t_recv.at[step], dev(to, xy))
+        rows = pl.ds(pl.multiple_of(q * 2 * nxy, 2 * nxy), 2 * nxy)
+        return rcopy(ret_s.at[to], ret_r.at[rows], t_send.at[step], t_recv.at[step], dev(to, xy))
 
     def send_ret(step, carry):
         ret_copy(step).start()
@@ -348,10 +431,10 @@
         return carry
 
     lax.fori_loop(1, nq, send_ret, 0)
-    ret_r[q] = ret_s[q]
+    ret_r[pl.ds(pl.multiple_of(q * 2 * nxy, 2 * nxy), 2 * nxy), :] = ret_s[q]
     lax.fori_loop(1, nq, wait_ret, 0)
-    back = ret_r[...].reshape(nq * 2, nxy, 128)
-    fin_s[...] = jnp.transpose(back, (1, 0, 2))
+    for at in range(nxy):
+        fin_s[at] = ret_r[pl.ds(at, 2 * nq, stride=nxy), :]
 
     def fin_copy(step):
         to = xy_peer(step)
@@ -367,6 +450,8 @@
 
     lax.fori_loop(1, nxy, send_fin, 0)
     fin_r[xy] = fin_s[xy]
+    for copy in sent + [up_half, down_half, up_full, down_full]:
+        copy.wait_send()
     lax.fori_loop(1, nxy, wait_fin, 0)
     out_ref[...] = fin_r[...].reshape(lb, 128)
 
@@ -386,54 +471,53 @@
         out_ref[1, rows, :] = v_re * sinv + v_im * cosv
 
 
-def local(nxy, nq, side, src_position, src_weight, src_phase, block_box, block_count, node_rate, target_phase):
+def local(side, src_position, src_weight, src_phase, block_box, block_count, node_rate, target_phase):
     slots, points = src_phase.shape
     lb = node_rate.shape[0]
-    ndev = nxy * nq
-    payload = pl.pallas_call(
-        leaf_kernel,
-        out_shape=jax.ShapeDtypeStruct((slots + 8, 128), F32),
-        in_specs=[VMEM, VMEM, VMEM, VMEM, SMEM],
+    nxy, nq = 16, 8
+    dma = pltpu.SemaphoreType.DMA
+    any_space = pl.BlockSpec(memory_space=pltpu.HBM)
+    state = pl.pallas_call(
+        butterfly_kernel,
+        out_shape=jax.ShapeDtypeStruct((lb, 128), F32),
+        in_specs=[any_space] * 6 + [VMEM, SMEM],
         out_specs=VMEM,
         scratch_shapes=[
+            pltpu.VMEM((2 * slots, points), F32),
+            pltpu.VMEM((2 * slots, points), F32),
+            pltpu.VMEM((slots, points), F32),
+            pltpu.VMEM((64, lb), F32),
+            pltpu.VMEM((256, 256), BF16),
+            pltpu.VMEM((256, 256), BF16),
             pltpu.VMEM((16, points, slots), F32),
             pltpu.VMEM((8, points, slots), F32),
             pltpu.VMEM((128, slots), F32),
-        ],
-        compiler_params=pltpu.CompilerParams(vmem_limit_bytes=32 * 2**20),
-        name="leaf",
-    )(src_position.reshape(2 * slots, points), src_weight.reshape(2 * slots, points), src_phase,
-      block_box.reshape(1, slots), block_count)
-
-    dma = pltpu.SemaphoreType.DMA
-    state = pl.pallas_call(
-        functools.partial(butterfly_kernel, nxy, nq),
-        out_shape=jax.ShapeDtypeStruct((lb, 128), F32),
-        in_specs=[VMEM] * 4,
-        out_specs=VMEM,
-        scratch_shapes=[
-            pltpu.VMEM((nxy, slots + 8, 128), F32),
+            pltpu.VMEM((nxy, 72, 128), F32),
+            pltpu.VMEM((nxy, 64, 128), F32),
             pltpu.VMEM((nxy * slots, 256), BF16),
-            pltpu.VMEM((nxy, nq, 128), F32),
-            pltpu.VMEM((nxy, nq, 128), F32),
+            pltpu.VMEM((nxy * nq, 128), F32),
+            pltpu.VMEM((nxy * nq, 128), F32),
             pltpu.VMEM((nq, nxy, 128), F32),
             pltpu.VMEM((nq, nxy, 128), F32),
             pltpu.VMEM((4, lb, 128), F32),
             pltpu.VMEM((4, lb, 128), F32),
             pltpu.VMEM((4, lb, 128), F32),
-            pltpu.VMEM((4, lb, 128), F32),
-            pltpu.VMEM((nq, 2, nxy, 128), F32),
-            pltpu.VMEM((nq, 2, nxy, 128), F32),
+            pltpu.VMEM((2, lb, 128), F32),
+            pltpu.VMEM((2, lb // 2, 128), F32),
+            pltpu.VMEM((nq, 2 * nxy, 128), F32),
+            pltpu.VMEM((lb, 128), F32),
             pltpu.VMEM((nxy, 2 * nq, 128), F32),
             pltpu.VMEM((nxy, 2 * nq, 128), F32),
-            dma((nxy,)), dma((nxy,)), dma((nxy,)), dma((nxy,)), dma((nq,)), dma((nq,)),
+            dma((6,)),
+            dma((2, 20)), dma((2, 20)), dma((nxy,)), dma((nxy,)), dma((nq,)), dma((nq,)),
             dma((4,)), dma((4,)), dma((4,)), dma((4,)),
             dma((nq,)), dma((nq,)), dma((nxy,)), dma((nxy,)),
         ],
         compiler_params=pltpu.CompilerParams(
-            collective_id=0, has_side_effects=True, vmem_limit_bytes=48 * 2**20),
+            collective_id=0, has_side_effects=True, vmem_limit_bytes=60 * 2**20),
         name="butterfly",
-    )(payload, node_rate, level_weight(0), level_weight(1))
+    )(src_position.reshape(2 * slots, points), src_weight.reshape(2 * slots, points), src_phase, node_rate.T,
+      level_weight(0), level_weight(1), block_box.reshape(1, slots), block_count)
 
     return pl.pallas_call(
         target_kernel,
@@ -446,7 +530,6 @@
 
 
 def solution(mesh):
-    n_hi, n_lo = mesh.shape["hi"], mesh.shape["lo"]
     placed = (
         P(("hi", "lo"), None, None),
         P(("hi", "lo"), None, None),
@@ -457,6 +540,6 @@
         P(("hi", "lo"), None),
     )
     return jax.shard_map(
-        functools.partial(local, n_lo // 2, 2 * n_hi, 16),
+        functools.partial(local, 16),
         mesh=mesh, in_specs=placed, out_specs=P(None, ("hi", "lo"), None), check_vma=False
     )

time: 55.5 us -> 49.2 us (0.89)
  Pallas kernels: 51.1 us -> 47.4 us
  local copies, waits for them, and re-layouts: 3.41 us -> 0.91 us
    pallas_call x2 -> x1, Pallas kernels: 49.9 us -> 46.2 us  [local(): pl.pallas_call(butterfly_kernel, out_shape=jax.ShapeDtypeStruct((lb, 128)...]
    unnamed x19 -> x6, local copies, waits for them, and re-layouts: 3.41 us -> 0.91 us
where the time goes in v2:
time: 49.2 us; the launch traced here: 49 us
  Pallas kernels  47.4 us (96%)
  local copies, waits for them, and re-layouts  0.91 us (2%)
  between operations  0.7 us (1%)
    pallas_call x1, Pallas kernels, local(): pl.pallas_call(butterfly_kernel, out_shape=jax.ShapeDtypeStruct((lb, 128)...  46.2 us
    pallas_call x1, Pallas kernels, local(): pl.pallas_call(target_kernel, out_shape=jax.ShapeDtypeStruct((2, lb, targ...  1.23 us

profile of v2, /device:TPU:1, one launch (start us, length us, event | category | flops | bytes accessed | tf_op | source)
XLA Modules:
  0.0 49.0 jit_solution(17361382766355449335)
XLA Ops:
  0.7 0.0 copy-start.1
  0.7 0.0 copy-start.2
  0.7 46.2 %butterfly.1.state_ref = f32[256,128]{1,0:T(8,128)} custom-call(f32[256,128]{1,0:T(8,128)} %bitcast.4, f32[256,128]{1,0:T(8,128)} %bitcast.5, f32[128,128]{1,0:T(8,128)} %phase_hbm.1, f32[64,256]{1,0:T(8,128)} %bitcast.6, bf16[256,256]{1,0:T(8,128)(2,1)} %constant.6.clone.w0_hbm, bf16[256,256]{1,0:T(8,128)(2,1)} %constant.7.clone.w1_hbm, s32[1,128]{1,0:T(1,128)} %bitcast.7, ...), custom_call_target="tpu_custom_call" | custom-call | tf_op jit(solution)/shard_map/butterfly/pallas_call | solution.py:480
  46.9 0.0 copy-done.1
  46.9 0.0 copy-done.2
  46.9 0.0 copy-start
  46.9 0.9 %copy-done = f32[256,128]{1,0:T(8,128)S(1)} copy-done((f32[256,128]{1,0:T(8,128)S(1)}, f32[256,128]{1,0:T(8,128)}, u32[]{:S(2)}) %copy-start) | copy-done | bytes 131096
  47.8 1.2 %target.1 = f32[2,256,256]{2,1,0:T(8,128)} custom-call(f32[256,128]{1,0:T(8,128)S(1)} %copy-done, f32[256,256]{1,0:T(8,128)S(1)} %copy-done.2, bf16[384,512]{1,0:T(8,128)(2,1)S(1)} %copy-done.1), custom_call_target="tpu_custom_call" | custom-call | tf_op jit(solution)/shard_map/target/pallas_call | solution.py:522
Async XLA Ops:
  0.7 46.2 %copy-start.1 = (bf16[384,512]{1,0:T(8,128)(2,1)S(1)}, bf16[384,512]{1,0:T(8,128)(2,1)}, u32[]{:S(2)}) copy-start(bf16[384,512]{1,0:T(8,128)(2,1)} %constant.8.clone.table_ref) | copy-start | bytes 1179652
  0.7 46.2 %copy-start.2 = (f32[256,256]{1,0:T(8,128)S(1)}, f32[256,256]{1,0:T(8,128)}, u32[]{:S(2)}) copy-start(f32[256,256]{1,0:T(8,128)} %phase_ref.1) | copy-start | bytes 786436
  46.9 0.9 %copy-start = (f32[256,128]{1,0:T(8,128)S(1)}, f32[256,128]{1,0:T(8,128)}, u32[]{:S(2)}) copy-start(f32[256,128]{1,0:T(8,128)} %butterfly.1.state_ref) | copy-start | bytes 393220

commit v3 on v2

--- a/solution.py
+++ b/solution.py
@@ -128,7 +128,7 @@
     return ct[...].T
 
 
-def butterfly_kernel(pos_hbm, wgt_hbm, phase_hbm, rate_hbm, w0_hbm, w1_hbm, box_ref, count_ref, out_ref,
+def exact_kernel(pos_hbm, wgt_hbm, phase_hbm, rate_hbm, w0_hbm, w1_hbm, box_ref, count_ref, out_ref,
                      pos_ref, wgt_ref, phase_ref, rate_ref, w0_ref, w1_ref, gx, ly, ct,
                      gath_a, gath_b, cat, rate_s, rate_r, rate_s2, rate_r2,
                      sib_s, sib_r, own, zrecv, z2recv, ret_s, ret_r, fin_s, fin_r,
@@ -456,6 +456,276 @@
     out_ref[...] = fin_r[...].reshape(lb, 128)
 
 
+S1, S2 = 40, 24
+M1, M2 = S1 + 16, S2 + 8
+
+
+def nt_dot(left, right):
+    return lax.dot_general(left, right, (((1,), (1,)), ((), ())), preferred_element_type=F32)
+
+
+def hot(cond):
+    return jnp.where(cond, 1.0, 0.0)
+
+
+def slot_kernel(pos_hbm, wgt_hbm, phase_hbm, rate_hbm, w0_hbm, w1_hbm, box_ref, count_ref, out_ref, flag_ref,
+                pos_ref, wgt_ref, phase_ref, rate_ref, w0_ref, w1_ref, gx, ly, ct,
+                rate_s, msg1_s, msg1_r, cat2, msg2_s, msg2_r, ret_s, ret_r, fin_s, fin_r,
+                in_sem, a_send, a_recv, c_send, c_recv, t_send, t_recv, f_send, f_recv):
+    nxy, nq = 16, 8
+    ndev = nxy * nq
+    lb = 2 * ndev
+    lx = 4
+    slots = 128
+    lbits = lb.bit_length() - 1
+    dbits = ndev.bit_length() - 1
+    hi = lax.axis_index("hi")
+    lo = lax.axis_index("lo")
+    xy = lax.div(lo, 2)
+    q = hi * 2 + lax.rem(lo, 2)
+
+    loads = [
+        pltpu.make_async_copy(src, dst, in_sem.at[i])
+        for i, (src, dst) in enumerate([
+            (phase_hbm, phase_ref), (wgt_hbm, wgt_ref), (pos_hbm, pos_ref),
+            (rate_hbm, rate_ref), (w0_hbm, w0_ref), (w1_hbm, w1_ref)])
+    ]
+    for load in loads:
+        load.start()
+
+    def dev(q_at, xy_at):
+        return lax.div(q_at, 2), xy_at * 2 + lax.rem(q_at, 2)
+
+    def xy_peer(step):
+        return lax.rem(xy + step, nxy)
+
+    def q_peer(step):
+        return lax.rem(q + step, nq)
+
+    def rcopy(src, dst, send, recv, target):
+        return pltpu.make_async_remote_copy(
+            src_ref=src, dst_ref=dst, send_sem=send, recv_sem=recv,
+            device_id=target, device_id_type=MESH)
+
+    barrier = pltpu.get_barrier_semaphore()
+
+    def greet_xy(step, carry):
+        pl.semaphore_signal(barrier, inc=1, device_id=dev(q, xy_peer(step)), device_id_type=MESH)
+        return carry
+
+    def greet_q(step, carry):
+        pl.semaphore_signal(barrier, inc=1, device_id=dev(q_peer(step), xy), device_id_type=MESH)
+        return carry
+
+    lax.fori_loop(1, nq, greet_q, 0)
+    lax.fori_loop(1, nxy, greet_xy, 0)
+
+    lane = lax.broadcasted_iota(jnp.int32, (1, slots), 1)
+    n = jnp.where(lane < count_ref[0], box_ref[...], -1)
+    j = n & (lb - 1)
+    owner = n >> lbits
+    holder = j & (ndev - 1)
+    q_d = ((owner >> (lx + 1)) << 1) | (owner & 1)
+    xy_d = (owner >> 1) & (nxy - 1)
+    row_at = ((j >> dbits) << dbits) + q_d * nxy + xy_d
+    live = n >= 0
+    q_to = jnp.where(live, holder & (nq - 1), -1)
+    before = hot(lax.broadcasted_iota(jnp.int32, (slots, slots), 0) < lax.broadcasted_iota(jnp.int32, (slots, slots), 1))
+    before = before.astype(BF16)
+    row128 = lax.broadcasted_iota(jnp.int32, (128, 128), 0)
+
+    to_q = hot(q_to == lax.broadcasted_iota(jnp.int32, (16, slots), 0))
+    ahead = jnp.dot(to_q.astype(BF16), before, preferred_element_type=F32)
+    rank = jnp.sum(to_q * ahead, axis=0, keepdims=True).astype(jnp.int32)
+    slot = jnp.where(live & (rank < S1 - 1), q_to * S1 + rank, -1)
+    names = jnp.concatenate([to_q * ((holder >> 3) + 1).astype(F32), to_q * row_at.astype(F32)], axis=0)
+    named = nt_dot(names.astype(BF16), hot(rank == row128).astype(BF16))
+    named = named[0:8] * 256.0 + named[16:24]
+    place = hot(slot == lax.broadcasted_iota(jnp.int32, (nq * S1, slots), 0)).astype(BF16)
+
+    for load in loads[0:4]:
+        load.wait()
+    rate_s[...] = jnp.concatenate([rate_ref[:, 0:ndev], rate_ref[:, ndev:lb]], axis=0).T
+    zeros = jnp.zeros((16, 256), BF16)
+    for at in range(nq):
+        cat2[at * 64 + 48:at * 64 + 64, :] = zeros
+    coeff = leaf(pos_ref, wgt_ref, phase_ref, gx, ly, ct)
+    both = jnp.dot(place, jnp.concatenate(split(coeff), axis=1), preferred_element_type=F32)
+    both = both[:, 0:128] + both[:, 128:256]
+    for at in range(nq):
+        msg1_s[at, 0:S1] = both[at * S1:(at + 1) * S1]
+        msg1_s[at, S1 - 1:S1] = named[at:at + 1]
+        msg1_s[at, S1:M1] = rate_s[pl.ds(at, nxy, stride=nq), :]
+    pl.semaphore_wait(barrier, nxy - 1 + nq - 1)
+
+    def first_copy(step):
+        to = q_peer(step)
+        rows = pl.ds(pl.multiple_of(q * M1, 8), M1)
+        return rcopy(msg1_s.at[to], msg1_r.at[rows], a_send.at[step], a_recv.at[step], dev(to, xy))
+
+    def send_first(step, carry):
+        first_copy(step).start()
+        return carry
+
+    def wait_first(step, carry):
+        first_copy(step).wait()
+        return carry
+
+    lax.fori_loop(1, nq, send_first, 0)
+    msg1_r[pl.ds(pl.multiple_of(q * M1, 8), M1), :] = msg1_s[q]
+    lax.fori_loop(1, nq, wait_first, 0)
+
+    meta = msg1_r[pl.ds(S1 - 1, nq, stride=M1), :]
+    lanes8 = lax.broadcasted_iota(jnp.int32, (nq, 128), 1)
+    over = jnp.max(jnp.where(lanes8 >= S1 - 1, meta, 0.0), axis=(0, 1), keepdims=True)
+    meta = jnp.where(lanes8 < S1 - 1, meta, 0.0)
+    odd = (lax.broadcasted_iota(jnp.int32, (nq, 128), 0) & 1) == 1
+    meta = jnp.where(odd, pltpu.roll(meta, 64, 1), meta)
+    codes = [(meta[2 * g:2 * g + 1] + meta[2 * g + 1:2 * g + 2]).astype(jnp.int32) for g in range(4)]
+    xy_to = [code >> 8 for code in codes]
+    row_to = [((code & 255) + 1).astype(F32) for code in codes]
+    id16 = lax.broadcasted_iota(jnp.int32, (nxy, 128), 0) + 1
+    to_xy = [hot(value == id16) for value in xy_to]
+    counted = jnp.dot(jnp.concatenate(to_xy, axis=0).astype(BF16),
+                      jnp.concatenate([before, jnp.ones((128, 128), BF16)], axis=1), preferred_element_type=F32)
+    ranks = []
+    total = jnp.zeros((nxy, 128), F32)
+    for g in range(4):
+        part = counted[g * nxy:(g + 1) * nxy]
+        ranks.append(jnp.sum(to_xy[g] * (part[:, 0:128] + total), axis=0, keepdims=True).astype(jnp.int32))
+        total = total + part[:, 128:256]
+    place_id = lax.broadcasted_iota(jnp.int32, (nxy * S2, 128), 0)
+    place2 = []
+    for g in range(4):
+        slot = jnp.where((xy_to[g] > 0) & (ranks[g] < S2 - 1), (xy_to[g] - 1) * S2 + ranks[g], -1)
+        place2.append(hot(slot == place_id).astype(BF16))
+    for at in range(nq):
+        high, low = split(msg1_r[at * M1:at * M1 + 48, :])
+        cat2[at * 64:at * 64 + 48, 0:128] = high
+        cat2[at * 64:at * 64 + 48, 128:256] = low
+    both = jnp.dot(jnp.concatenate(place2, axis=1), cat2[...], preferred_element_type=F32)
+    both = both[:, 0:128] + both[:, 128:256]
+    names = jnp.concatenate([to_xy[g] * row_to[g] for g in range(4)], axis=1)
+    named = nt_dot(names.astype(BF16), jnp.concatenate([hot(ranks[g] == row128).astype(BF16) for g in range(4)], axis=1))
+    lanes16 = lax.broadcasted_iota(jnp.int32, (nxy, 128), 1)
+    named = named + jnp.where((lanes16 == 127) & (over > 0.0), 1.0, 0.0)
+    for at in range(nxy):
+        msg2_s[at, 0:S2] = both[at * S2:(at + 1) * S2]
+        msg2_s[at, S2 - 1:S2] = named[at:at + 1]
+        msg2_s[at, S2:M2] = msg1_r[pl.ds(S1 + at, nq, stride=M1), :]
+
+    def second_copy(step):
+        to = xy_peer(step)
+        rows = pl.ds(pl.multiple_of(xy * M2, M2), M2)
+        return rcopy(msg2_s.at[to], msg2_r.at[rows], c_send.at[step], c_recv.at[step], dev(q, to))
+
+    def send_second(step, carry):
+        second_copy(step).start()
+        return carry
+
+    def wait_second(step, carry):
+        second_copy(step).wait()
+        return carry
+
+    lax.fori_loop(1, nxy, send_second, 0)
+    msg2_r[pl.ds(pl.multiple_of(xy * M2, M2), M2), :] = msg2_s[xy]
+    for load in loads[4:6]:
+        load.wait()
+    lax.fori_loop(1, nxy, wait_second, 0)
+
+    meta = msg2_r[pl.ds(S2 - 1, nxy, stride=M2), :]
+    over = jnp.max(jnp.where(lanes16 >= S2 - 1, meta, 0.0), axis=(0, 1), keepdims=True)
+    mark = jnp.where(over > 0.0, jnp.nan, 0.0)
+    meta = jnp.where(lanes16 < S2 - 1, meta, 0.0)
+    sub4 = lax.broadcasted_iota(jnp.int32, (nxy, 128), 0) & 3
+    for turn in range(1, 4):
+        meta = jnp.where(sub4 == turn, pltpu.roll(meta, 32 * turn, 1), meta)
+    row_id = lax.broadcasted_iota(jnp.int32, (lb, 128), 0)
+    put = []
+    for g in range(4):
+        code = jnp.sum(meta[4 * g:4 * g + 4], axis=0, keepdims=True).astype(jnp.int32) - 1
+        put.append(hot(code == row_id).astype(BF16))
+    both = jnp.dot(jnp.concatenate(put, axis=1), jnp.concatenate(split(msg2_r[...]), axis=1), preferred_element_type=F32)
+    state = both[:, 0:128] + both[:, 128:256]
+
+    rates = jnp.concatenate([msg2_r[pl.ds(S2 + at, nxy, stride=M2), :] for at in range(nq)], axis=0)
+    sin_p, cos_p = sincos(rates)
+    left = lax.broadcasted_iota(jnp.int32, (ndev, 128), 1) < 64
+    cos_o = pltpu.roll(cos_p, 64, 1)
+    sin_o = pltpu.roll(sin_p, 64, 1)
+    cos1 = jnp.concatenate([jnp.where(left, cos_p, cos_o), jnp.where(left, cos_o, cos_p)], axis=0)
+    sin1 = jnp.concatenate([jnp.where(left, -sin_p, sin_o), jnp.where(left, -sin_o, sin_p)], axis=0)
+
+    cosv, sinv = cos1, sin1
+    sub = lax.broadcasted_iota(jnp.int32, (lb // 8, 8, 128), 1)
+    for step in range(dbits):
+        if step > 0:
+            cosv, sinv = cosv * cos1 - sinv * sin1, sinv * cos1 + cosv * sin1
+        bit = lx if step == 0 else (step - 1 if step <= lx else step)
+        if bit < 3:
+            tiles = state.reshape(lb // 8, 8, 128)
+            dist = 1 << bit
+            upper = (sub & dist) != 0
+            first = jnp.where(upper, pltpu.roll(tiles, dist, 1), tiles).reshape(lb, 128)
+            second = jnp.where(upper, tiles, pltpu.roll(tiles, 8 - dist, 1)).reshape(lb, 128)
+        else:
+            pairs = state.reshape(lb >> (bit + 1), 2, 1 << bit, 128)
+            first = jnp.concatenate([pairs[:, 0:1], pairs[:, 0:1]], axis=1).reshape(lb, 128)
+            second = jnp.concatenate([pairs[:, 1:2], pairs[:, 1:2]], axis=1).reshape(lb, 128)
+        first = cosv * first + sinv * pltpu.roll(first, 64, 1)
+        second = cosv * second + sinv * pltpu.roll(second, 64, 1)
+        high, low = split(jnp.concatenate([first, second], axis=1))
+        w_ref = w0_ref if step % 2 == 0 else w1_ref
+        main = jnp.dot(high, w_ref[...], preferred_element_type=F32)
+        rest = jnp.dot(low, w_ref[:, 0:128], preferred_element_type=F32)
+        state = main[:, 0:128] + (main[:, 128:256] + rest)
+
+    state = state + mark
+
+    for at in range(nq):
+        for jj in range(2):
+            base = jj * ndev + at * nxy
+            ret_s[at, jj * nxy:(jj + 1) * nxy] = state[base:base + nxy]
+
+    def ret_copy(step):
+        to = q_peer(step)
+        rows = pl.ds(pl.multiple_of(q * 2 * nxy, 2 * nxy), 2 * nxy)
+        return rcopy(ret_s.at[to], ret_r.at[rows], t_send.at[step], t_recv.at[step], dev(to, xy))
+
+    def send_ret(step, carry):
+        ret_copy(step).start()
+        return carry
+
+    def wait_ret(step, carry):
+        ret_copy(step).wait()
+        return carry
+
+    lax.fori_loop(1, nq, send_ret, 0)
+    ret_r[pl.ds(pl.multiple_of(q * 2 * nxy, 2 * nxy), 2 * nxy), :] = ret_s[q]
+    lax.fori_loop(1, nq, wait_ret, 0)
+    for at in range(nxy):
+        fin_s[at] = ret_r[pl.ds(at, 2 * nq, stride=nxy), :]
+
+    def fin_copy(step):
+        to = xy_peer(step)
+        return rcopy(fin_s.at[to], fin_r.at[xy], f_send.at[step], f_recv.at[step], dev(q, to))
+
+    def send_fin(step, carry):
+        fin_copy(step).start()
+        return carry
+
+    def wait_fin(step, carry):
+        fin_copy(step).wait()
+        return carry
+
+    lax.fori_loop(1, nxy, send_fin, 0)
+    fin_r[xy] = fin_s[xy]
+    lax.fori_loop(1, nxy, wait_fin, 0)
+    result = fin_r[...].reshape(lb, 128)
+    out_ref[...] = result
+    flag_ref[0] = jnp.max(jnp.where(result != result, 1.0, 0.0)).astype(jnp.int32)
+
+
 def target_kernel(state_ref, phase_ref, table_ref, out_ref):
     lb, points = phase_ref.shape
     half = lb // 2
@@ -476,57 +746,91 @@
     lb = node_rate.shape[0]
     nxy, nq = 16, 8
     dma = pltpu.SemaphoreType.DMA
-    any_space = pl.BlockSpec(memory_space=pltpu.HBM)
-    state = pl.pallas_call(
-        butterfly_kernel,
-        out_shape=jax.ShapeDtypeStruct((lb, 128), F32),
-        in_specs=[any_space] * 6 + [VMEM, SMEM],
-        out_specs=VMEM,
-        scratch_shapes=[
-            pltpu.VMEM((2 * slots, points), F32),
-            pltpu.VMEM((2 * slots, points), F32),
-            pltpu.VMEM((slots, points), F32),
-            pltpu.VMEM((64, lb), F32),
-            pltpu.VMEM((256, 256), BF16),
-            pltpu.VMEM((256, 256), BF16),
-            pltpu.VMEM((16, points, slots), F32),
-            pltpu.VMEM((8, points, slots), F32),
-            pltpu.VMEM((128, slots), F32),
-            pltpu.VMEM((nxy, 72, 128), F32),
-            pltpu.VMEM((nxy, 64, 128), F32),
-            pltpu.VMEM((nxy * slots, 256), BF16),
+    hbm = pl.BlockSpec(memory_space=pltpu.HBM)
+    operands = (
+        src_position.reshape(2 * slots, points), src_weight.reshape(2 * slots, points), src_phase, node_rate.T,
+        level_weight(0), level_weight(1), block_box.reshape(1, slots), block_count)
+    held = [
+        pltpu.VMEM((2 * slots, points), F32),
+        pltpu.VMEM((2 * slots, points), F32),
+        pltpu.VMEM((slots, points), F32),
+        pltpu.VMEM((64, lb), F32),
+        pltpu.VMEM((256, 256), BF16),
+        pltpu.VMEM((256, 256), BF16),
+        pltpu.VMEM((16, points, slots), F32),
+        pltpu.VMEM((8, points, slots), F32),
+        pltpu.VMEM((128, slots), F32),
+    ]
+    returned = [
+        pltpu.VMEM((nq, 2 * nxy, 128), F32),
+        pltpu.VMEM((lb, 128), F32),
+        pltpu.VMEM((nxy, 2 * nq, 128), F32),
+        pltpu.VMEM((nxy, 2 * nq, 128), F32),
+    ]
+    state_shape = jax.ShapeDtypeStruct((lb, 128), F32)
+
+    def exact():
+        return pl.pallas_call(
+            exact_kernel,
+            out_shape=state_shape,
+            in_specs=[hbm] * 6 + [VMEM, SMEM],
+            out_specs=VMEM,
+            scratch_shapes=held + [
+                pltpu.VMEM((nxy, 72, 128), F32),
+                pltpu.VMEM((nxy, 64, 128), F32),
+                pltpu.VMEM((nxy * slots, 256), BF16),
+                pltpu.VMEM((nxy * nq, 128), F32),
+                pltpu.VMEM((nxy * nq, 128), F32),
+                pltpu.VMEM((nq, nxy, 128), F32),
+                pltpu.VMEM((nq, nxy, 128), F32),
+                pltpu.VMEM((4, lb, 128), F32),
+                pltpu.VMEM((4, lb, 128), F32),
+                pltpu.VMEM((4, lb, 128), F32),
+                pltpu.VMEM((2, lb, 128), F32),
+                pltpu.VMEM((2, lb // 2, 128), F32),
+            ] + returned + [
+                dma((6,)),
+                dma((2, 20)), dma((2, 20)), dma((nxy,)), dma((nxy,)), dma((nq,)), dma((nq,)),
+                dma((4,)), dma((4,)), dma((4,)), dma((4,)),
+                dma((nq,)), dma((nq,)), dma((nxy,)), dma((nxy,)),
+            ],
+            compiler_params=pltpu.CompilerParams(
+                collective_id=1, has_side_effects=True, vmem_limit_bytes=60 * 2**20),
+            name="exact",
+        )(*operands)
+
+    def targets(state):
+        return pl.pallas_call(
+            target_kernel,
+            out_shape=jax.ShapeDtypeStruct((2, lb, target_phase.shape[1]), F32),
+            in_specs=[VMEM] * 3,
+            out_specs=VMEM,
+            compiler_params=pltpu.CompilerParams(vmem_limit_bytes=32 * 2**20),
+            name="target",
+        )(state, target_phase, target_weight(side))
+
+    state, flag = pl.pallas_call(
+        slot_kernel,
+        out_shape=(state_shape, jax.ShapeDtypeStruct((1,), jnp.int32)),
+        in_specs=[hbm] * 6 + [VMEM, SMEM],
+        out_specs=(VMEM, SMEM),
+        scratch_shapes=held + [
             pltpu.VMEM((nxy * nq, 128), F32),
-            pltpu.VMEM((nxy * nq, 128), F32),
-            pltpu.VMEM((nq, nxy, 128), F32),
-            pltpu.VMEM((nq, nxy, 128), F32),
-            pltpu.VMEM((4, lb, 128), F32),
-            pltpu.VMEM((4, lb, 128), F32),
-            pltpu.VMEM((4, lb, 128), F32),
-            pltpu.VMEM((2, lb, 128), F32),
-            pltpu.VMEM((2, lb // 2, 128), F32),
-            pltpu.VMEM((nq, 2 * nxy, 128), F32),
-            pltpu.VMEM((lb, 128), F32),
-            pltpu.VMEM((nxy, 2 * nq, 128), F32),
-            pltpu.VMEM((nxy, 2 * nq, 128), F32),
+            pltpu.VMEM((nq, M1, 128), F32),
+            pltpu.VMEM((nq * M1, 128), F32),
+            pltpu.VMEM((nq * 64, 256), BF16),
+            pltpu.VMEM((nxy, M2, 128), F32),
+            pltpu.VMEM((nxy * M2, 128), F32),
+        ] + returned + [
             dma((6,)),
-            dma((2, 20)), dma((2, 20)), dma((nxy,)), dma((nxy,)), dma((nq,)), dma((nq,)),
-            dma((4,)), dma((4,)), dma((4,)), dma((4,)),
+            dma((nq,)), dma((nq,)), dma((nxy,)), dma((nxy,)),
             dma((nq,)), dma((nq,)), dma((nxy,)), dma((nxy,)),
         ],
         compiler_params=pltpu.CompilerParams(
             collective_id=0, has_side_effects=True, vmem_limit_bytes=60 * 2**20),
-        name="butterfly",
-    )(src_position.reshape(2 * slots, points), src_weight.reshape(2 * slots, points), src_phase, node_rate.T,
-      level_weight(0), level_weight(1), block_box.reshape(1, slots), block_count)
-
-    return pl.pallas_call(
-        target_kernel,
-        out_shape=jax.ShapeDtypeStruct((2, lb, target_phase.shape[1]), F32),
-        in_specs=[VMEM] * 3,
-        out_specs=VMEM,
-        compiler_params=pltpu.CompilerParams(vmem_limit_bytes=32 * 2**20),
-        name="target",
-    )(state, target_phase, target_weight(side))
+        name="slots",
+    )(*operands)
+    return lax.cond(flag[0] > 0, lambda: targets(exact()), lambda: targets(state))
 
 
 def solution(mesh):

time: 49.2 us -> 35.3 us (0.72)
  Pallas kernels: 47.4 us -> 32.2 us
  between operations: 0.7 us -> 1.44 us
  local copies, waits for them, and re-layouts: 0.91 us -> 1.43 us
    pallas_call x2, Pallas kernels: 47.4 us -> 32.2 us  [the longest x1 31.8 us: local(): pl.pallas_call(slot_kernel, out_shape=(state_shape, jax.ShapeDtypeStruct(...]
    unnamed x6 -> x8, local copies, waits for them, and re-layouts: 0.91 us -> 1.43 us
where the time goes in v3:
time: 35.3 us; the launch traced here: 35.1 us
  Pallas kernels  32.2 us (91%)
  between operations  1.44 us (4%)
  local copies, waits for them, and re-layouts  1.43 us (4%)
    pallas_call x1, Pallas kernels, local(): pl.pallas_call(slot_kernel, out_shape=(state_shape, jax.ShapeDtypeStruct(...  31.8 us
    unnamed x8, local copies, waits for them, and re-layouts  1.43 us

profile of v3, /device:TPU:1, one launch (start us, length us, event | category | flops | bytes accessed | tf_op | source)
XLA Modules:
  0.0 35.1 jit_solution(15283678636939643306)
XLA Ops:
  0.0 0.0 copy-start.1
  0.7 0.0 copy-start.2
  0.7 31.8 %slots.1 = (f32[256,128]{1,0:T(8,128)S(1)}, s32[1]{0:T(128)}) custom-call(f32[256,128]{1,0:T(8,128)} %bitcast.5, f32[256,128]{1,0:T(8,128)} %bitcast.7, f32[128,128]{1,0:T(8,128)} %phase_hbm.1, f32[64,256]{1,0:T(8,128)} %bitcast.9, bf16[256,256]{1,0:T(8,128)(2,1)} %constant.9.clone.w0_hbm, bf16[256,256]{1,0:T(8,128)(2,1)} %constant.10.clone.w1_hbm, ...), custom_call_target="tpu_custom_call" | custom-call | tf_op jit(solution)/shard_map/slots/pallas_call | solution.py:812
  33.2 0.0 copy-start.4
  33.2 0.0 copy-done.1
  33.2 0.0 copy-done.2
  33.2 0.6 %copy-done.4 = s32[128]{0:T(128)S(1)} copy-done((s32[128]{0:T(128)S(1)}, s32[128]{0:T(128)}, u32[]{:S(2)}) %copy-start.4) | copy-done | bytes 536
  33.9 0.4 %conditional.1 = (f32[2,256,256]{2,1,0:T(8,128)S(1)}) conditional(s32[]{:T(128)} %bitcast.4, (f32[256,128]{1,0:T(8,128)S(1)}, f32[256,256]{1,0:T(8,128)S(1)}, bf16[384,512]{1,0:T(8,128)(2,1)S(1)}) %tuple.19, (f32[256,128]{1,0:T(8,128)}, f32[256,128]{1,0:T(8,128)}, f32[128,128]{1,0:T(8,128)}, f32[64,256]{1,0:T(8,128)}, bf16[256,256]{1,0:T(8,128)(2,1)}, ...), branch_computations={%region_0.0_spmd, %region_1.0_spmd} | conditional | bytes 524324 | solution.py:833
  33.9 0.4 %target.2 = f32[2,256,256]{2,1,0:T(8,128)S(1)} custom-call(f32[256,128]{1,0:T(8,128)S(1)} %get-tuple-element.34.state_ref, f32[256,256]{1,0:T(8,128)S(1)} %get-tuple-element.35.phase_ref, bf16[384,512]{1,0:T(8,128)(2,1)S(1)} %get-tuple-element.36.table_ref), custom_call_target="tpu_custom_call" | custom-call | tf_op jit(solution)/shard_map/cond/branch_0_fun/target/pallas_call | solution.py:803
  34.3 0.0 copy-start.3
  34.3 0.8 %copy-done.3 = f32[2,256,256]{2,1,0:T(8,128)} copy-done((f32[2,256,256]{2,1,0:T(8,128)}, f32[2,256,256]{2,1,0:T(8,128)S(1)}, u32[]{:S(2)}) %copy-start.3) | copy-done | bytes 524312
Async XLA Ops:
  0.0 33.2 %copy-start.1 = (bf16[384,512]{1,0:T(8,128)(2,1)S(1)}, bf16[384,512]{1,0:T(8,128)(2,1)}, u32[]{:S(2)}) copy-start(bf16[384,512]{1,0:T(8,128)(2,1)} %constant.11.clone) | copy-start | bytes 1179652
  0.7 32.5 %copy-start.2 = (f32[256,256]{1,0:T(8,128)S(1)}, f32[256,256]{1,0:T(8,128)}, u32[]{:S(2)}) copy-start(f32[256,256]{1,0:T(8,128)} %param.19) | copy-start | bytes 786436
  33.2 0.7 %copy-start.4 = (s32[128]{0:T(128)S(1)}, s32[128]{0:T(128)}, u32[]{:S(2)}) copy-start(s32[128]{0:T(128)} %param.16) | copy-start | bytes 1540
  34.3 0.8 %copy-start.3 = (f32[2,256,256]{2,1,0:T(8,128)}, f32[2,256,256]{2,1,0:T(8,128)S(1)}, u32[]{:S(2)}) copy-start(f32[2,256,256]{2,1,0:T(8,128)S(1)} %get-tuple-element.54) | copy-start | bytes 1572868

commit v4 on v3

--- a/solution.py
+++ b/solution.py
@@ -128,7 +128,7 @@
     return ct[...].T
 
 
-def exact_kernel(pos_hbm, wgt_hbm, phase_hbm, rate_hbm, w0_hbm, w1_hbm, box_ref, count_ref, out_ref,
+def exact_kernel(pos_hbm, wgt_hbm, phase_hbm, rate_hbm, w0_hbm, w1_hbm, key_ref, out_ref,
                      pos_ref, wgt_ref, phase_ref, rate_ref, w0_ref, w1_ref, gx, ly, ct,
                      gath_a, gath_b, cat, rate_s, rate_r, rate_s2, rate_r2,
                      sib_s, sib_r, own, zrecv, z2recv, ret_s, ret_r, fin_s, fin_r,
@@ -191,8 +191,7 @@
     for load in loads[0:3]:
         load.wait()
     coeff = leaf(pos_ref, wgt_ref, phase_ref, gx, ly, ct)
-    lane = lax.broadcasted_iota(jnp.int32, (1, slots), 1)
-    key = jnp.where(lane < count_ref[0], box_ref[...], -1).astype(F32)
+    key = key_ref[...].astype(F32)
     gath_a[y_at * 4 + x_at, 0:64, :] = coeff[64:128]
     gath_a[y_at * 4 + x_at, 64:72, :] = jnp.broadcast_to(key, (8, slots))
     gath_b[x_at * 4 + y_at] = coeff[0:64]
@@ -460,6 +459,15 @@
 M1, M2 = S1 + 16, S2 + 8
 
 
+def far(step, size):
+    return min(step, size - step)
+
+
+XY_STEPS = sorted(range(1, 16), key=lambda s: -far(s // 4, 4) - far(s % 4, 4))
+Q_STEPS = sorted(range(1, 8), key=lambda s: -far(s // 4 * 2 + s % 2, 4))
+ALL_STEPS = sorted(range(1, 128), key=lambda s: -far(s // 64 * 2 + s % 2, 4) - far(s // 8 % 4, 4) - far(s // 2 % 4, 4))
+
+
 def nt_dot(left, right):
     return lax.dot_general(left, right, (((1,), (1,)), ((), ())), preferred_element_type=F32)
 
@@ -468,14 +476,13 @@
     return jnp.where(cond, 1.0, 0.0)
 
 
-def slot_kernel(pos_hbm, wgt_hbm, phase_hbm, rate_hbm, w0_hbm, w1_hbm, box_ref, count_ref, out_ref, flag_ref,
-                pos_ref, wgt_ref, phase_ref, rate_ref, w0_ref, w1_ref, gx, ly, ct,
-                rate_s, msg1_s, msg1_r, cat2, msg2_s, msg2_r, ret_s, ret_r, fin_s, fin_r,
-                in_sem, a_send, a_recv, c_send, c_recv, t_send, t_recv, f_send, f_recv):
+def slot_kernel(pos_hbm, wgt_hbm, phase_hbm, rate_hbm, w0_hbm, w1_hbm, box_hbm, count_ref, out_ref, flag_ref, key_ref,
+                pos_ref, wgt_ref, phase_ref, rate_ref, w0_ref, w1_ref, box_ref, gx, ly, ct,
+                rate_s, msg1_s, msg1_r, cat2, msg2_s, msg2_r, cos_s, sin_s, ret_s, ret_r,
+                in_sem, a_send, a_recv, c_send, c_recv, t_send, t_recv):
     nxy, nq = 16, 8
     ndev = nxy * nq
     lb = 2 * ndev
-    lx = 4
     slots = 128
     lbits = lb.bit_length() - 1
     dbits = ndev.bit_length() - 1
@@ -484,50 +491,43 @@
     xy = lax.div(lo, 2)
     q = hi * 2 + lax.rem(lo, 2)
 
+    def dev(q_at, xy_at):
+        return lax.div(q_at, 2), xy_at * 2 + lax.rem(q_at, 2)
+
+    def xy_peer(step):
+        return lax.rem(xy + step, nxy)
+
+    def q_peer(step):
+        return lax.rem(q + step, nq)
+
+    def rcopy(src, dst, send, recv, target):
+        return pltpu.make_async_remote_copy(
+            src_ref=src, dst_ref=dst, send_sem=send, recv_sem=recv,
+            device_id=target, device_id_type=MESH)
+
+    barrier = pltpu.get_barrier_semaphore()
+    for step in XY_STEPS:
+        pl.semaphore_signal(barrier, inc=1, device_id=dev(q, xy_peer(step)), device_id_type=MESH)
+    for step in Q_STEPS:
+        pl.semaphore_signal(barrier, inc=1, device_id=dev(q_peer(step), xy), device_id_type=MESH)
+
     loads = [
         pltpu.make_async_copy(src, dst, in_sem.at[i])
         for i, (src, dst) in enumerate([
-            (phase_hbm, phase_ref), (wgt_hbm, wgt_ref), (pos_hbm, pos_ref),
+            (box_hbm, box_ref), (phase_hbm, phase_ref), (wgt_hbm, wgt_ref), (pos_hbm, pos_ref),
             (rate_hbm, rate_ref), (w0_hbm, w0_ref), (w1_hbm, w1_ref)])
     ]
     for load in loads:
         load.start()
 
-    def dev(q_at, xy_at):
-        return lax.div(q_at, 2), xy_at * 2 + lax.rem(q_at, 2)
-
-    def xy_peer(step):
-        return lax.rem(xy + step, nxy)
-
-    def q_peer(step):
-        return lax.rem(q + step, nq)
-
-    def rcopy(src, dst, send, recv, target):
-        return pltpu.make_async_remote_copy(
-            src_ref=src, dst_ref=dst, send_sem=send, recv_sem=recv,
-            device_id=target, device_id_type=MESH)
-
-    barrier = pltpu.get_barrier_semaphore()
-
-    def greet_xy(step, carry):
-        pl.semaphore_signal(barrier, inc=1, device_id=dev(q, xy_peer(step)), device_id_type=MESH)
-        return carry
-
-    def greet_q(step, carry):
-        pl.semaphore_signal(barrier, inc=1, device_id=dev(q_peer(step), xy), device_id_type=MESH)
-        return carry
-
-    lax.fori_loop(1, nq, greet_q, 0)
-    lax.fori_loop(1, nxy, greet_xy, 0)
-
+    loads[0].wait()
     lane = lax.broadcasted_iota(jnp.int32, (1, slots), 1)
     n = jnp.where(lane < count_ref[0], box_ref[...], -1)
+    key_ref[...] = n
     j = n & (lb - 1)
     owner = n >> lbits
     holder = j & (ndev - 1)
-    q_d = ((owner >> (lx + 1)) << 1) | (owner & 1)
-    xy_d = (owner >> 1) & (nxy - 1)
-    row_at = ((j >> dbits) << dbits) + q_d * nxy + xy_d
+    row_at = owner * 2 + (j >> dbits)
     live = n >= 0
     q_to = jnp.where(live, holder & (nq - 1), -1)
     before = hot(lax.broadcasted_iota(jnp.int32, (slots, slots), 0) < lax.broadcasted_iota(jnp.int32, (slots, slots), 1))
@@ -543,7 +543,7 @@
     named = named[0:8] * 256.0 + named[16:24]
     place = hot(slot == lax.broadcasted_iota(jnp.int32, (nq * S1, slots), 0)).astype(BF16)
 
-    for load in loads[0:4]:
+    for load in loads[1:5]:
         load.wait()
     rate_s[...] = jnp.concatenate([rate_ref[:, 0:ndev], rate_ref[:, ndev:lb]], axis=0).T
     zeros = jnp.zeros((16, 256), BF16)
@@ -563,17 +563,11 @@
         rows = pl.ds(pl.multiple_of(q * M1, 8), M1)
         return rcopy(msg1_s.at[to], msg1_r.at[rows], a_send.at[step], a_recv.at[step], dev(to, xy))
 
-    def send_first(step, carry):
+    for step in Q_STEPS:
         first_copy(step).start()
-        return carry
-
-    def wait_first(step, carry):
-        first_copy(step).wait()
-        return carry
-
-    lax.fori_loop(1, nq, send_first, 0)
     msg1_r[pl.ds(pl.multiple_of(q * M1, 8), M1), :] = msg1_s[q]
-    lax.fori_loop(1, nq, wait_first, 0)
+    for step in reversed(Q_STEPS):
+        first_copy(step).wait_recv()
 
     meta = msg1_r[pl.ds(S1 - 1, nq, stride=M1), :]
     lanes8 = lax.broadcasted_iota(jnp.int32, (nq, 128), 1)
@@ -619,19 +613,13 @@
         rows = pl.ds(pl.multiple_of(xy * M2, M2), M2)
         return rcopy(msg2_s.at[to], msg2_r.at[rows], c_send.at[step], c_recv.at[step], dev(q, to))
 
-    def send_second(step, carry):
+    for step in XY_STEPS:
         second_copy(step).start()
-        return carry
-
-    def wait_second(step, carry):
-        second_copy(step).wait()
-        return carry
-
-    lax.fori_loop(1, nxy, send_second, 0)
     msg2_r[pl.ds(pl.multiple_of(xy * M2, M2), M2), :] = msg2_s[xy]
-    for load in loads[4:6]:
+    for load in loads[5:7]:
         load.wait()
-    lax.fori_loop(1, nxy, wait_second, 0)
+    for step in reversed(XY_STEPS):
+        second_copy(step).wait_recv()
 
     meta = msg2_r[pl.ds(S2 - 1, nxy, stride=M2), :]
     over = jnp.max(jnp.where(lanes16 >= S2 - 1, meta, 0.0), axis=(0, 1), keepdims=True)
@@ -653,15 +641,25 @@
     left = lax.broadcasted_iota(jnp.int32, (ndev, 128), 1) < 64
     cos_o = pltpu.roll(cos_p, 64, 1)
     sin_o = pltpu.roll(sin_p, 64, 1)
-    cos1 = jnp.concatenate([jnp.where(left, cos_p, cos_o), jnp.where(left, cos_o, cos_p)], axis=0)
-    sin1 = jnp.concatenate([jnp.where(left, -sin_p, sin_o), jnp.where(left, -sin_o, sin_p)], axis=0)
+    for at in range(nq):
+        rows = slice(at * nxy, (at + 1) * nxy)
+        base = 2 * (at // 2 * 2 * nxy + at % 2)
+        even = pl.ds(base, nxy, stride=4)
+        uneven = pl.ds(base + 1, nxy, stride=4)
+        lr = left[rows]
+        cos_s[even, :] = jnp.where(lr, cos_p[rows], cos_o[rows])
+        cos_s[uneven, :] = jnp.where(lr, cos_o[rows], cos_p[rows])
+        sin_s[even, :] = jnp.where(lr, -sin_p[rows], sin_o[rows])
+        sin_s[uneven, :] = jnp.where(lr, -sin_o[rows], sin_p[rows])
+    cos1 = cos_s[...]
+    sin1 = sin_s[...]
 
     cosv, sinv = cos1, sin1
     sub = lax.broadcasted_iota(jnp.int32, (lb // 8, 8, 128), 1)
     for step in range(dbits):
         if step > 0:
             cosv, sinv = cosv * cos1 - sinv * sin1, sinv * cos1 + cosv * sin1
-        bit = lx if step == 0 else (step - 1 if step <= lx else step)
+        bit = step + 1
         if bit < 3:
             tiles = state.reshape(lb // 8, 8, 128)
             dist = 1 << bit
@@ -682,48 +680,27 @@
 
     state = state + mark
 
-    for at in range(nq):
-        for jj in range(2):
-            base = jj * ndev + at * nxy
-            ret_s[at, jj * nxy:(jj + 1) * nxy] = state[base:base + nxy]
+    ret_s[...] = state.reshape(ndev, 2, 128)
+    holder_at = xy * nq + q
 
     def ret_copy(step):
-        to = q_peer(step)
-        rows = pl.ds(pl.multiple_of(q * 2 * nxy, 2 * nxy), 2 * nxy)
-        return rcopy(ret_s.at[to], ret_r.at[rows], t_send.at[step], t_recv.at[step], dev(to, xy))
-
-    def send_ret(step, carry):
+        hi_to = lax.rem(hi + step // 32, 4)
+        lo_to = lax.rem(lo + step % 32, 32)
+        return rcopy(ret_s.at[hi_to * 32 + lo_to], ret_r.at[holder_at], t_send, t_recv, (hi_to, lo_to))
+
+    for step in ALL_STEPS:
         ret_copy(step).start()
-        return carry
-
-    def wait_ret(step, carry):
-        ret_copy(step).wait()
-        return carry
-
-    lax.fori_loop(1, nq, send_ret, 0)
-    ret_r[pl.ds(pl.multiple_of(q * 2 * nxy, 2 * nxy), 2 * nxy), :] = ret_s[q]
-    lax.fori_loop(1, nq, wait_ret, 0)
-    for at in range(nxy):
-        fin_s[at] = ret_r[pl.ds(at, 2 * nq, stride=nxy), :]
-
-    def fin_copy(step):
-        to = xy_peer(step)
-        return rcopy(fin_s.at[to], fin_r.at[xy], f_send.at[step], f_recv.at[step], dev(q, to))
-
-    def send_fin(step, carry):
-        fin_copy(step).start()
-        return carry
-
-    def wait_fin(step, carry):
-        fin_copy(step).wait()
-        return carry
-
-    lax.fori_loop(1, nxy, send_fin, 0)
-    fin_r[xy] = fin_s[xy]
-    lax.fori_loop(1, nxy, wait_fin, 0)
-    result = fin_r[...].reshape(lb, 128)
+    ret_r[holder_at] = ret_s[hi * 32 + lo]
+    for step in Q_STEPS:
+        first_copy(step).wait_send()
+    for step in XY_STEPS:
+        second_copy(step).wait_send()
+    every = rcopy(ret_s.at[0:ndev - 1], ret_r.at[0:ndev - 1], t_send, t_recv, dev(q_peer(1), xy))
+    every.wait_recv()
+    result = ret_r[...]
     out_ref[...] = result
     flag_ref[0] = jnp.max(jnp.where(result != result, 1.0, 0.0)).astype(jnp.int32)
+    every.wait_send()
 
 
 def target_kernel(state_ref, phase_ref, table_ref, out_ref):
@@ -757,6 +734,7 @@
         pltpu.VMEM((64, lb), F32),
         pltpu.VMEM((256, 256), BF16),
         pltpu.VMEM((256, 256), BF16),
+        pltpu.VMEM((1, slots), jnp.int32),
         pltpu.VMEM((16, points, slots), F32),
         pltpu.VMEM((8, points, slots), F32),
         pltpu.VMEM((128, slots), F32),
@@ -769,13 +747,13 @@
     ]
     state_shape = jax.ShapeDtypeStruct((lb, 128), F32)
 
-    def exact():
+    def exact(key):
         return pl.pallas_call(
             exact_kernel,
             out_shape=state_shape,
-            in_specs=[hbm] * 6 + [VMEM, SMEM],
+            in_specs=[hbm] * 6 + [VMEM],
             out_specs=VMEM,
-            scratch_shapes=held + [
+            scratch_shapes=held[0:6] + held[7:] + [
                 pltpu.VMEM((nxy, 72, 128), F32),
                 pltpu.VMEM((nxy, 64, 128), F32),
                 pltpu.VMEM((nxy * slots, 256), BF16),
@@ -797,7 +775,7 @@
             compiler_params=pltpu.CompilerParams(
                 collective_id=1, has_side_effects=True, vmem_limit_bytes=60 * 2**20),
             name="exact",
-        )(*operands)
+        )(*operands[0:6], key)
 
     def targets(state):
         return pl.pallas_call(
@@ -809,11 +787,12 @@
             name="target",
         )(state, target_phase, target_weight(side))
 
-    state, flag = pl.pallas_call(
+    state, flag, key = pl.pallas_call(
         slot_kernel,
-        out_shape=(state_shape, jax.ShapeDtypeStruct((1,), jnp.int32)),
-        in_specs=[hbm] * 6 + [VMEM, SMEM],
-        out_specs=(VMEM, SMEM),
+        out_shape=(jax.ShapeDtypeStruct((lb // 2, 2, 128), F32), jax.ShapeDtypeStruct((1,), jnp.int32),
+                   jax.ShapeDtypeStruct((1, slots), jnp.int32)),
+        in_specs=[hbm] * 7 + [SMEM],
+        out_specs=(VMEM, SMEM, VMEM),
         scratch_shapes=held + [
             pltpu.VMEM((nxy * nq, 128), F32),
             pltpu.VMEM((nq, M1, 128), F32),
@@ -821,16 +800,19 @@
             pltpu.VMEM((nq * 64, 256), BF16),
             pltpu.VMEM((nxy, M2, 128), F32),
             pltpu.VMEM((nxy * M2, 128), F32),
-        ] + returned + [
-            dma((6,)),
-            dma((nq,)), dma((nq,)), dma((nxy,)), dma((nxy,)),
-            dma((nq,)), dma((nq,)), dma((nxy,)), dma((nxy,)),
+            pltpu.VMEM((lb, 128), F32),
+            pltpu.VMEM((lb, 128), F32),
+            pltpu.VMEM((nxy * nq, 2, 128), F32),
+            pltpu.VMEM((nxy * nq, 2, 128), F32),
+            dma((7,)),
+            dma((nq,)), dma((nq,)), dma((nxy,)), dma((nxy,)), dma, dma,
         ],
         compiler_params=pltpu.CompilerParams(
             collective_id=0, has_side_effects=True, vmem_limit_bytes=60 * 2**20),
         name="slots",
     )(*operands)
-    return lax.cond(flag[0] > 0, lambda: targets(exact()), lambda: targets(state))
+    state = state.reshape(lb, 128)
+    return lax.cond(flag[0] > 0, lambda: targets(exact(key)), lambda: targets(state))
 
 
 def solution(mesh):

time: 35.3 us -> 31.6 us (0.90)
  Pallas kernels: 32.2 us -> 29.4 us
  local copies, waits for them, and re-layouts: 1.43 us -> 0.8 us
    pallas_call x1, Pallas kernels: 31.8 us -> 28.9 us  [local(): pl.pallas_call(slot_kernel, out_shape=(jax.ShapeDtypeStruct((lb // 2, 2,...]
    unnamed x8 -> x6, local copies, waits for them, and re-layouts: 1.43 us -> 0.8 us
where the time goes in v4:
time: 31.6 us; the launch traced here: 31.5 us
  Pallas kernels  29.4 us (93%)
  between operations  1.31 us (4%)
  local copies, waits for them, and re-layouts  0.8 us (3%)
    pallas_call x1, Pallas kernels, local(): pl.pallas_call(slot_kernel, out_shape=(jax.ShapeDtypeStruct((lb // 2, 2,...  28.9 us
    unnamed x6, local copies, waits for them, and re-layouts  0.8 us

profile of v4, /device:TPU:1, one launch (start us, length us, event | category | flops | bytes accessed | tf_op | source)
XLA Modules:
  0.0 31.5 jit_solution(13422473384467344596)
XLA Ops:
  0.0 0.0 copy-start.1
  0.7 0.0 copy-start.2
  0.7 28.9 %slots.1 = (f32[128,2,128]{2,1,0:T(2,128)S(1)}, s32[1]{0:T(128)}, s32[1,128]{1,0:T(1,128)S(1)}) custom-call(f32[256,128]{1,0:T(8,128)} %bitcast.6, f32[256,128]{1,0:T(8,128)} %bitcast.8, f32[128,128]{1,0:T(8,128)} %phase_hbm.1, f32[64,256]{1,0:T(8,128)} %bitcast.10, bf16[256,256]{1,0:T(8,128)(2,1)} %constant.9.clone.w0_hbm, ...), custom_call_target="tpu_custom_call" | custom-call | tf_op jit(solution)/shard_map/slots/pallas_call | solution.py:790
  30.2 0.0 copy-done.1
  30.2 0.0 copy-done.2
  30.2 0.5 %conditional.1 = (f32[2,256,256]{2,1,0:T(8,128)S(1)}) conditional(s32[]{:T(128)} %bitcast.5, (f32[128,2,128]{2,1,0:T(2,128)S(1)}, f32[256,256]{1,0:T(8,128)S(1)}, bf16[384,512]{1,0:T(8,128)(2,1)S(1)}) %tuple.19, (f32[256,128]{1,0:T(8,128)}, f32[256,128]{1,0:T(8,128)}, f32[128,128]{1,0:T(8,128)}, f32[64,256]{1,0:T(8,128)}, bf16[256,256]{1,0:T(8,128)(2,1)}, ...), branch_computations={%region_0.0_spmd, %region_1.0_spmd} | conditional | bytes 524324 | solution.py:815
  30.2 0.4 %target.2 = f32[2,256,256]{2,1,0:T(8,128)S(1)} custom-call(f32[256,128]{1,0:T(8,128)S(1)} %bitcast.12, f32[256,256]{1,0:T(8,128)S(1)} %get-tuple-element.34.phase_ref, bf16[384,512]{1,0:T(8,128)(2,1)S(1)} %get-tuple-element.35.table_ref), custom_call_target="tpu_custom_call" | custom-call | tf_op jit(solution)/shard_map/cond/branch_0_fun/target/pallas_call | solution.py:781
  30.7 0.0 copy-start.3
  30.7 0.8 %copy-done.3 = f32[2,256,256]{2,1,0:T(8,128)} copy-done((f32[2,256,256]{2,1,0:T(8,128)}, f32[2,256,256]{2,1,0:T(8,128)S(1)}, u32[]{:S(2)}) %copy-start.3) | copy-done | bytes 524312
Async XLA Ops:
  0.0 30.2 %copy-start.1 = (bf16[384,512]{1,0:T(8,128)(2,1)S(1)}, bf16[384,512]{1,0:T(8,128)(2,1)}, u32[]{:S(2)}) copy-start(bf16[384,512]{1,0:T(8,128)(2,1)} %constant.11.clone) | copy-start | bytes 1179652
  0.7 29.5 %copy-start.2 = (f32[256,256]{1,0:T(8,128)S(1)}, f32[256,256]{1,0:T(8,128)}, u32[]{:S(2)}) copy-start(f32[256,256]{1,0:T(8,128)} %param.19) | copy-start | bytes 786436
  30.7 0.8 %copy-start.3 = (f32[2,256,256]{2,1,0:T(8,128)}, f32[2,256,256]{2,1,0:T(8,128)S(1)}, u32[]{:S(2)}) copy-start(f32[2,256,256]{2,1,0:T(8,128)S(1)} %get-tuple-element.54) | copy-start | bytes 1572868

commit v5 on v4

--- a/solution.py
+++ b/solution.py
@@ -456,7 +456,6 @@
 
 
 S1, S2 = 40, 24
-M1, M2 = S1 + 16, S2 + 8
 
 
 def far(step, size):
@@ -476,10 +475,11 @@
     return jnp.where(cond, 1.0, 0.0)
 
 
-def slot_kernel(pos_hbm, wgt_hbm, phase_hbm, rate_hbm, w0_hbm, w1_hbm, box_hbm, count_ref, out_ref, flag_ref, key_ref,
-                pos_ref, wgt_ref, phase_ref, rate_ref, w0_ref, w1_ref, box_ref, gx, ly, ct,
-                rate_s, msg1_s, msg1_r, cat2, msg2_s, msg2_r, cos_s, sin_s, ret_s, ret_r,
-                in_sem, a_send, a_recv, c_send, c_recv, t_send, t_recv):
+def slot_kernel(pos_hbm, wgt_hbm, phase_hbm, rate_hbm, w0_hbm, w1_hbm, box_hbm, count_hbm, target_hbm,
+                out_ref, flag_ref, key_ref, cos_out, sin_out,
+                pos_ref, wgt_ref, phase_ref, rate_ref, w0_ref, w1_ref, box_ref, count_ref, target_ref, gx, ly, ct,
+                rate_s, rate_r, rate_s2, rate_r2, msg1_s, msg1_r, cat2, msg2_s, msg2_r, cos_s, sin_s, ret_s, ret_r,
+                in_sem, a_send, a_recv, c_send, c_recv, r_send, r_recv, r2_send, r2_recv, t_send, t_recv):
     nxy, nq = 16, 8
     ndev = nxy * nq
     lb = 2 * ndev
@@ -515,19 +515,23 @@
         pltpu.make_async_copy(src, dst, in_sem.at[i])
         for i, (src, dst) in enumerate([
             (box_hbm, box_ref), (phase_hbm, phase_ref), (wgt_hbm, wgt_ref), (pos_hbm, pos_ref),
-            (rate_hbm, rate_ref), (w0_hbm, w0_ref), (w1_hbm, w1_ref)])
+            (rate_hbm, rate_ref), (w0_hbm, w0_ref), (w1_hbm, w1_ref), (target_hbm, target_ref),
+            (count_hbm, count_ref)])
     ]
-    for load in loads:
+    for load in loads[8:] + loads[:8]:
         load.start()
 
+    loads[8].wait()
     loads[0].wait()
     lane = lax.broadcasted_iota(jnp.int32, (1, slots), 1)
-    n = jnp.where(lane < count_ref[0], box_ref[...], -1)
+    n = jnp.where(lane < count_ref[...], box_ref[...], -1)
     key_ref[...] = n
     j = n & (lb - 1)
     owner = n >> lbits
     holder = j & (ndev - 1)
-    row_at = owner * 2 + (j >> dbits)
+    q_d = ((owner >> 5) << 1) | (owner & 1)
+    xy_d = (owner >> 1) & (nxy - 1)
+    row_at = ((j >> dbits) << dbits) + q_d * nxy + xy_d
     live = n >= 0
     q_to = jnp.where(live, holder & (nq - 1), -1)
     before = hot(lax.broadcasted_iota(jnp.int32, (slots, slots), 0) < lax.broadcasted_iota(jnp.int32, (slots, slots), 1))
@@ -553,23 +557,44 @@
     both = jnp.dot(place, jnp.concatenate(split(coeff), axis=1), preferred_element_type=F32)
     both = both[:, 0:128] + both[:, 128:256]
     for at in range(nq):
-        msg1_s[at, 0:S1] = both[at * S1:(at + 1) * S1]
-        msg1_s[at, S1 - 1:S1] = named[at:at + 1]
-        msg1_s[at, S1:M1] = rate_s[pl.ds(at, nxy, stride=nq), :]
+        msg1_s[at * S1:(at + 1) * S1] = both[at * S1:(at + 1) * S1]
+        msg1_s[(at + 1) * S1 - 1:(at + 1) * S1] = named[at:at + 1]
     pl.semaphore_wait(barrier, nxy - 1 + nq - 1)
+
+    def slot_rows(at, size):
+        return pl.ds(pl.multiple_of(at * size, 8), size)
 
     def first_copy(step):
         to = q_peer(step)
-        rows = pl.ds(pl.multiple_of(q * M1, 8), M1)
-        return rcopy(msg1_s.at[to], msg1_r.at[rows], a_send.at[step], a_recv.at[step], dev(to, xy))
+        return rcopy(msg1_s.at[slot_rows(to, S1)], msg1_r.at[slot_rows(q, S1)], a_send, a_recv, dev(to, xy))
+
+    def rate_copy(step):
+        to = xy_peer(step)
+        return rcopy(rate_s.at[slot_rows(to, nq)], rate_r.at[slot_rows(xy, nq)], r_send, r_recv, dev(q, to))
+
+    def rate2_copy(step):
+        to = q_peer(step)
+        return rcopy(rate_s2.at[to], rate_r2.at[q], r2_send, r2_recv, dev(to, xy))
+
+    first_all = rcopy(msg1_s.at[0:(nq - 1) * S1], msg1_r.at[0:(nq - 1) * S1], a_send, a_recv, dev(q_peer(1), xy))
+    second_all = rcopy(msg2_s.at[0:(nxy - 1) * S2], msg2_r.at[0:(nxy - 1) * S2], c_send, c_recv, dev(q, xy_peer(1)))
+    rate_all = rcopy(rate_s.at[0:(nxy - 1) * nq], rate_r.at[0:(nxy - 1) * nq], r_send, r_recv, dev(q, xy_peer(1)))
+    rate2_all = rcopy(rate_s2.at[0:nq - 1], rate_r2.at[0:nq - 1], r2_send, r2_recv, dev(q_peer(1), xy))
 
     for step in Q_STEPS:
         first_copy(step).start()
-    msg1_r[pl.ds(pl.multiple_of(q * M1, 8), M1), :] = msg1_s[q]
-    for step in reversed(Q_STEPS):
-        first_copy(step).wait_recv()
-
-    meta = msg1_r[pl.ds(S1 - 1, nq, stride=M1), :]
+    for step in XY_STEPS:
+        rate_copy(step).start()
+    rate_r[slot_rows(xy, nq), :] = rate_s[slot_rows(xy, nq), :]
+    for load in loads[5:8]:
+        load.wait()
+    sin_t, cos_t = sincos(target_ref[...])
+    cos_out[...] = cos_t
+    sin_out[...] = sin_t
+    msg1_r[slot_rows(q, S1), :] = msg1_s[slot_rows(q, S1), :]
+    first_all.wait_recv()
+
+    meta = msg1_r[pl.ds(S1 - 1, nq, stride=S1), :]
     lanes8 = lax.broadcasted_iota(jnp.int32, (nq, 128), 1)
     over = jnp.max(jnp.where(lanes8 >= S1 - 1, meta, 0.0), axis=(0, 1), keepdims=True)
     meta = jnp.where(lanes8 < S1 - 1, meta, 0.0)
@@ -594,7 +619,8 @@
         slot = jnp.where((xy_to[g] > 0) & (ranks[g] < S2 - 1), (xy_to[g] - 1) * S2 + ranks[g], -1)
         place2.append(hot(slot == place_id).astype(BF16))
     for at in range(nq):
-        high, low = split(msg1_r[at * M1:at * M1 + 48, :])
+        rows = jnp.concatenate([msg1_r[at * S1:at * S1 + S1, :], jnp.zeros((48 - S1, 128), F32)], axis=0)
+        high, low = split(rows)
         cat2[at * 64:at * 64 + 48, 0:128] = high
         cat2[at * 64:at * 64 + 48, 128:256] = low
     both = jnp.dot(jnp.concatenate(place2, axis=1), cat2[...], preferred_element_type=F32)
@@ -604,24 +630,35 @@
     lanes16 = lax.broadcasted_iota(jnp.int32, (nxy, 128), 1)
     named = named + jnp.where((lanes16 == 127) & (over > 0.0), 1.0, 0.0)
     for at in range(nxy):
-        msg2_s[at, 0:S2] = both[at * S2:(at + 1) * S2]
-        msg2_s[at, S2 - 1:S2] = named[at:at + 1]
-        msg2_s[at, S2:M2] = msg1_r[pl.ds(S1 + at, nq, stride=M1), :]
+        msg2_s[at * S2:(at + 1) * S2] = both[at * S2:(at + 1) * S2]
+        msg2_s[(at + 1) * S2 - 1:(at + 1) * S2] = named[at:at + 1]
 
     def second_copy(step):
         to = xy_peer(step)
-        rows = pl.ds(pl.multiple_of(xy * M2, M2), M2)
-        return rcopy(msg2_s.at[to], msg2_r.at[rows], c_send.at[step], c_recv.at[step], dev(q, to))
+        return rcopy(msg2_s.at[slot_rows(to, S2)], msg2_r.at[slot_rows(xy, S2)], c_send, c_recv, dev(q, to))
 
     for step in XY_STEPS:
         second_copy(step).start()
-    msg2_r[pl.ds(pl.multiple_of(xy * M2, M2), M2), :] = msg2_s[xy]
-    for load in loads[5:7]:
-        load.wait()
-    for step in reversed(XY_STEPS):
-        second_copy(step).wait_recv()
-
-    meta = msg2_r[pl.ds(S2 - 1, nxy, stride=M2), :]
+    msg2_r[slot_rows(xy, S2), :] = msg2_s[slot_rows(xy, S2), :]
+    rate_all.wait_recv()
+    for at in range(nq):
+        rate_s2[at] = rate_r[pl.ds(at, nxy, stride=nq), :]
+    for step in Q_STEPS:
+        rate2_copy(step).start()
+    rate_r2[q] = rate_s2[q]
+    rate2_all.wait_recv()
+    rates = rate_r2[...].reshape(ndev, 128)
+    sin_p, cos_p = sincos(rates)
+    left = lax.broadcasted_iota(jnp.int32, (ndev, 128), 1) < 64
+    cos_o = pltpu.roll(cos_p, 64, 1)
+    sin_o = pltpu.roll(sin_p, 64, 1)
+    cos_s[0] = jnp.where(left, cos_p, cos_o)
+    cos_s[1] = jnp.where(left, cos_o, cos_p)
+    sin_s[0] = jnp.where(left, -sin_p, sin_o)
+    sin_s[1] = jnp.where(left, -sin_o, sin_p)
+    second_all.wait_recv()
+
+    meta = msg2_r[pl.ds(S2 - 1, nxy, stride=S2), :]
     over = jnp.max(jnp.where(lanes16 >= S2 - 1, meta, 0.0), axis=(0, 1), keepdims=True)
     mark = jnp.where(over > 0.0, jnp.nan, 0.0)
     meta = jnp.where(lanes16 < S2 - 1, meta, 0.0)
@@ -629,89 +666,85 @@
     for turn in range(1, 4):
         meta = jnp.where(sub4 == turn, pltpu.roll(meta, 32 * turn, 1), meta)
     row_id = lax.broadcasted_iota(jnp.int32, (lb, 128), 0)
+    spread = []
+    for at in range(nxy):
+        spread += [msg2_r[at * S2:(at + 1) * S2, :], jnp.zeros((32 - S2, 128), F32)]
+    spread = jnp.concatenate(spread, axis=0)
     put = []
     for g in range(4):
         code = jnp.sum(meta[4 * g:4 * g + 4], axis=0, keepdims=True).astype(jnp.int32) - 1
         put.append(hot(code == row_id).astype(BF16))
-    both = jnp.dot(jnp.concatenate(put, axis=1), jnp.concatenate(split(msg2_r[...]), axis=1), preferred_element_type=F32)
+    both = jnp.dot(jnp.concatenate(put, axis=1), jnp.concatenate(split(spread), axis=1), preferred_element_type=F32)
     state = both[:, 0:128] + both[:, 128:256]
 
-    rates = jnp.concatenate([msg2_r[pl.ds(S2 + at, nxy, stride=M2), :] for at in range(nq)], axis=0)
-    sin_p, cos_p = sincos(rates)
-    left = lax.broadcasted_iota(jnp.int32, (ndev, 128), 1) < 64
-    cos_o = pltpu.roll(cos_p, 64, 1)
-    sin_o = pltpu.roll(sin_p, 64, 1)
-    for at in range(nq):
-        rows = slice(at * nxy, (at + 1) * nxy)
-        base = 2 * (at // 2 * 2 * nxy + at % 2)
-        even = pl.ds(base, nxy, stride=4)
-        uneven = pl.ds(base + 1, nxy, stride=4)
-        lr = left[rows]
-        cos_s[even, :] = jnp.where(lr, cos_p[rows], cos_o[rows])
-        cos_s[uneven, :] = jnp.where(lr, cos_o[rows], cos_p[rows])
-        sin_s[even, :] = jnp.where(lr, -sin_p[rows], sin_o[rows])
-        sin_s[uneven, :] = jnp.where(lr, -sin_o[rows], sin_p[rows])
-    cos1 = cos_s[...]
-    sin1 = sin_s[...]
-
-    cosv, sinv = cos1, sin1
-    sub = lax.broadcasted_iota(jnp.int32, (lb // 8, 8, 128), 1)
+    sub = lax.broadcasted_iota(jnp.int32, (ndev // 8, 8, 128), 1)
+    states = [state[0:ndev], state[ndev:lb]]
+    cosv = [cos_s[0], cos_s[1]]
+    sinv = [sin_s[0], sin_s[1]]
     for step in range(dbits):
-        if step > 0:
-            cosv, sinv = cosv * cos1 - sinv * sin1, sinv * cos1 + cosv * sin1
-        bit = step + 1
-        if bit < 3:
-            tiles = state.reshape(lb // 8, 8, 128)
-            dist = 1 << bit
-            upper = (sub & dist) != 0
-            first = jnp.where(upper, pltpu.roll(tiles, dist, 1), tiles).reshape(lb, 128)
-            second = jnp.where(upper, tiles, pltpu.roll(tiles, 8 - dist, 1)).reshape(lb, 128)
-        else:
-            pairs = state.reshape(lb >> (bit + 1), 2, 1 << bit, 128)
-            first = jnp.concatenate([pairs[:, 0:1], pairs[:, 0:1]], axis=1).reshape(lb, 128)
-            second = jnp.concatenate([pairs[:, 1:2], pairs[:, 1:2]], axis=1).reshape(lb, 128)
-        first = cosv * first + sinv * pltpu.roll(first, 64, 1)
-        second = cosv * second + sinv * pltpu.roll(second, 64, 1)
-        high, low = split(jnp.concatenate([first, second], axis=1))
+        bit = 4 if step == 0 else (step - 1 if step <= 4 else step)
         w_ref = w0_ref if step % 2 == 0 else w1_ref
-        main = jnp.dot(high, w_ref[...], preferred_element_type=F32)
-        rest = jnp.dot(low, w_ref[:, 0:128], preferred_element_type=F32)
-        state = main[:, 0:128] + (main[:, 128:256] + rest)
-
-    state = state + mark
-
-    ret_s[...] = state.reshape(ndev, 2, 128)
+        for jj in range(2):
+            state = states[jj]
+            if step > 0:
+                cosv[jj], sinv[jj] = (cosv[jj] * cos_s[jj] - sinv[jj] * sin_s[jj],
+                                      sinv[jj] * cos_s[jj] + cosv[jj] * sin_s[jj])
+            if bit < 3:
+                tiles = state.reshape(ndev // 8, 8, 128)
+                dist = 1 << bit
+                upper = (sub & dist) != 0
+                first = jnp.where(upper, pltpu.roll(tiles, dist, 1), tiles).reshape(ndev, 128)
+                second = jnp.where(upper, tiles, pltpu.roll(tiles, 8 - dist, 1)).reshape(ndev, 128)
+            else:
+                pairs = state.reshape(ndev >> (bit + 1), 2, 1 << bit, 128)
+                first = jnp.concatenate([pairs[:, 0:1], pairs[:, 0:1]], axis=1).reshape(ndev, 128)
+                second = jnp.concatenate([pairs[:, 1:2], pairs[:, 1:2]], axis=1).reshape(ndev, 128)
+            first = cosv[jj] * first + sinv[jj] * pltpu.roll(first, 64, 1)
+            second = cosv[jj] * second + sinv[jj] * pltpu.roll(second, 64, 1)
+            high, low = split(jnp.concatenate([first, second], axis=1))
+            main = jnp.dot(high, w_ref[...], preferred_element_type=F32)
+            rest = jnp.dot(low, w_ref[:, 0:128], preferred_element_type=F32)
+            states[jj] = main[:, 0:128] + (main[:, 128:256] + rest)
+
+    for jj in range(2):
+        ret_s[pl.ds(jj, ndev, stride=2), :] = states[jj] + mark
     holder_at = xy * nq + q
 
-    def ret_copy(step):
-        hi_to = lax.rem(hi + step // 32, 4)
-        lo_to = lax.rem(lo + step % 32, 32)
-        return rcopy(ret_s.at[hi_to * 32 + lo_to], ret_r.at[holder_at], t_send, t_recv, (hi_to, lo_to))
-
-    for step in ALL_STEPS:
-        ret_copy(step).start()
-    ret_r[holder_at] = ret_s[hi * 32 + lo]
-    for step in Q_STEPS:
-        first_copy(step).wait_send()
-    for step in XY_STEPS:
-        second_copy(step).wait_send()
-    every = rcopy(ret_s.at[0:ndev - 1], ret_r.at[0:ndev - 1], t_send, t_recv, dev(q_peer(1), xy))
+    def ret_to(hi_step, lo_step):
+        hi_to = lax.rem(hi + hi_step, 4)
+        lo_to = lax.rem(lo + lo_step, 32)
+        at = (hi_to * 2 + lax.rem(lo_to, 2)) * nxy + lax.div(lo_to, 2)
+        return rcopy(ret_s.at[pl.ds(at * 2, 2)], ret_r.at[pl.ds(holder_at * 2, 2)], t_send, t_recv, (hi_to, lo_to))
+
+    def send_eight(block, carry):
+        for a in range(1, 4):
+            for b in range(8):
+                ret_to(a, block * 8 + b).start()
+        return carry
+
+    lax.fori_loop(0, 4, send_eight, 0)
+    for step in range(1, 32):
+        ret_to(0, step).start()
+    ret_r[pl.ds(holder_at * 2, 2), :] = ret_s[pl.ds((q * nxy + xy) * 2, 2), :]
+    every = rcopy(ret_s.at[0:lb - 2], ret_r.at[0:lb - 2], t_send, t_recv, dev(q_peer(1), xy))
     every.wait_recv()
     result = ret_r[...]
     out_ref[...] = result
-    flag_ref[0] = jnp.max(jnp.where(result != result, 1.0, 0.0)).astype(jnp.int32)
-    every.wait_send()
-
-
-def target_kernel(state_ref, phase_ref, table_ref, out_ref):
-    lb, points = phase_ref.shape
+    total = jnp.sum(result, axis=0, keepdims=True)
+    flag_ref[0] = jnp.max(jnp.where(total != total, 1.0, 0.0)).astype(jnp.int32)
+    for copy in (first_all, second_all, rate_all, rate2_all, every):
+        copy.wait_send()
+
+
+def target_kernel(state_ref, cos_ref, sin_ref, table_ref, out_ref):
+    lb, points = cos_ref.shape
     half = lb // 2
     for jj in range(2):
         rows = slice(jj * half, jj * half + half)
         high, low = split(state_ref[pl.ds(jj, half, stride=2), :])
         stacked = jnp.concatenate([high, low, high], axis=1)
         value = jnp.dot(stacked, table_ref[...], preferred_element_type=F32)
-        sinv, cosv = sincos(phase_ref[rows, :])
+        cosv, sinv = cos_ref[rows, :], sin_ref[rows, :]
         v_re = value[:, 0:points]
         v_im = value[:, points:2 * points]
         out_ref[0, rows, :] = v_re * cosv - v_im * sinv
@@ -726,7 +759,7 @@
     hbm = pl.BlockSpec(memory_space=pltpu.HBM)
     operands = (
         src_position.reshape(2 * slots, points), src_weight.reshape(2 * slots, points), src_phase, node_rate.T,
-        level_weight(0), level_weight(1), block_box.reshape(1, slots), block_count)
+        level_weight(0), level_weight(1), block_box.reshape(1, slots), block_count.reshape(1, 1), target_phase)
     held = [
         pltpu.VMEM((2 * slots, points), F32),
         pltpu.VMEM((2 * slots, points), F32),
@@ -735,6 +768,8 @@
         pltpu.VMEM((256, 256), BF16),
         pltpu.VMEM((256, 256), BF16),
         pltpu.VMEM((1, slots), jnp.int32),
+        pltpu.VMEM((1, 1), jnp.int32),
+        pltpu.VMEM(target_phase.shape, F32),
         pltpu.VMEM((16, points, slots), F32),
         pltpu.VMEM((8, points, slots), F32),
         pltpu.VMEM((128, slots), F32),
@@ -753,7 +788,7 @@
             out_shape=state_shape,
             in_specs=[hbm] * 6 + [VMEM],
             out_specs=VMEM,
-            scratch_shapes=held[0:6] + held[7:] + [
+            scratch_shapes=held[0:6] + held[9:] + [
                 pltpu.VMEM((nxy, 72, 128), F32),
                 pltpu.VMEM((nxy, 64, 128), F32),
                 pltpu.VMEM((nxy * slots, 256), BF16),
@@ -781,38 +816,41 @@
         return pl.pallas_call(
             target_kernel,
             out_shape=jax.ShapeDtypeStruct((2, lb, target_phase.shape[1]), F32),
-            in_specs=[VMEM] * 3,
+            in_specs=[VMEM] * 4,
             out_specs=VMEM,
             compiler_params=pltpu.CompilerParams(vmem_limit_bytes=32 * 2**20),
             name="target",
-        )(state, target_phase, target_weight(side))
-
-    state, flag, key = pl.pallas_call(
+        )(state, cosv, sinv, target_weight(side))
+
+    state, flag, key, cosv, sinv = pl.pallas_call(
         slot_kernel,
-        out_shape=(jax.ShapeDtypeStruct((lb // 2, 2, 128), F32), jax.ShapeDtypeStruct((1,), jnp.int32),
-                   jax.ShapeDtypeStruct((1, slots), jnp.int32)),
-        in_specs=[hbm] * 7 + [SMEM],
-        out_specs=(VMEM, SMEM, VMEM),
+        out_shape=(state_shape, jax.ShapeDtypeStruct((1,), jnp.int32),
+                   jax.ShapeDtypeStruct((1, slots), jnp.int32),
+                   jax.ShapeDtypeStruct(target_phase.shape, F32), jax.ShapeDtypeStruct(target_phase.shape, F32)),
+        in_specs=[hbm] * 9,
+        out_specs=(VMEM, SMEM, VMEM, VMEM, VMEM),
         scratch_shapes=held + [
             pltpu.VMEM((nxy * nq, 128), F32),
-            pltpu.VMEM((nq, M1, 128), F32),
-            pltpu.VMEM((nq * M1, 128), F32),
+            pltpu.VMEM((nxy * nq, 128), F32),
+            pltpu.VMEM((nq, nxy, 128), F32),
+            pltpu.VMEM((nq, nxy, 128), F32),
+            pltpu.VMEM((nq * S1, 128), F32),
+            pltpu.VMEM((nq * S1, 128), F32),
             pltpu.VMEM((nq * 64, 256), BF16),
-            pltpu.VMEM((nxy, M2, 128), F32),
-            pltpu.VMEM((nxy * M2, 128), F32),
+            pltpu.VMEM((nxy * S2, 128), F32),
+            pltpu.VMEM((nxy * S2, 128), F32),
+            pltpu.VMEM((2, lb // 2, 128), F32),
+            pltpu.VMEM((2, lb // 2, 128), F32),
             pltpu.VMEM((lb, 128), F32),
             pltpu.VMEM((lb, 128), F32),
-            pltpu.VMEM((nxy * nq, 2, 128), F32),
-            pltpu.VMEM((nxy * nq, 2, 128), F32),
-            dma((7,)),
-            dma((nq,)), dma((nq,)), dma((nxy,)), dma((nxy,)), dma, dma,
+            dma((9,)),
+            dma, dma, dma, dma, dma, dma, dma, dma, dma, dma,
         ],
         compiler_params=pltpu.CompilerParams(
             collective_id=0, has_side_effects=True, vmem_limit_bytes=60 * 2**20),
         name="slots",
     )(*operands)
-    state = state.reshape(lb, 128)
-    return lax.cond(flag[0] > 0, lambda: targets(exact(key)), lambda: targets(state))
+    return lax.switch(flag[0], (lambda: targets(state), lambda: targets(exact(key))))
 
 
 def solution(mesh):

time: 31.6 us -> 30.1 us (0.953)
  Pallas kernels: 29.4 us -> 27.7 us
    pallas_call x1, Pallas kernels: 28.9 us -> 27.4 us  [local(): pl.pallas_call(slot_kernel, out_shape=(state_shape, jax.ShapeDtypeStruct(...]
    unnamed x6 -> x12, local copies, waits for them, and re-layouts: 0.8 us -> 0.82 us
where the time goes in v5:
time: 30.1 us; the launch traced here: 29.9 us
  Pallas kernels  27.7 us (92%)
  between operations  1.39 us (5%)
  local copies, waits for them, and re-layouts  0.82 us (3%)
    pallas_call x1, Pallas kernels, local(): pl.pallas_call(slot_kernel, out_shape=(state_shape, jax.ShapeDtypeStruct(...  27.4 us
    unnamed x12, local copies, waits for them, and re-layouts  0.82 us

profile of v5, /device:TPU:1, one launch (start us, length us, event | category | flops | bytes accessed | tf_op | source)
XLA Modules:
  0.0 29.9 jit_solution(1888148963025591946)
XLA Ops:
  0.7 0.0 copy-start.1
  0.7 0.0 copy-start.3
  0.7 0.0 copy-start.4
  0.7 0.0 copy-start.5
  0.7 0.0 copy-start.6
  0.7 27.4 %slots.1 = (f32[256,128]{1,0:T(8,128)S(1)}, s32[1]{0:T(128)}, s32[1,128]{1,0:T(1,128)S(1)}, f32[256,256]{1,0:T(8,128)S(1)}, f32[256,256]{1,0:T(8,128)S(1)}) custom-call(f32[256,128]{1,0:T(8,128)} %bitcast.7, f32[256,128]{1,0:T(8,128)} %bitcast.9, f32[128,128]{1,0:T(8,128)} %phase_hbm.1, f32[64,256]{1,0:T(8,128)} %bitcast.11, ...), custom_call_target="tpu_custom_call" | custom-call | tf_op jit(solution)/shard_map/slots/pallas_call | solution.py:825
  28.8 0.0 copy-done.1
  28.8 0.0 copy-done.3
  28.8 0.0 copy-done.4
  28.8 0.0 copy-done.5
  28.8 0.0 copy-done.6
  28.8 0.3 %conditional.1 = (f32[2,256,256]{2,1,0:T(8,128)S(1)}) conditional(s32[]{:T(128)} %bitcast.5, (f32[256,128]{1,0:T(8,128)S(1)}, f32[256,256]{1,0:T(8,128)S(1)}, f32[256,256]{1,0:T(8,128)S(1)}, bf16[384,512]{1,0:T(8,128)(2,1)S(1)}) %tuple.17, (f32[256,128]{1,0:T(8,128)S(1)}, f32[256,128]{1,0:T(8,128)S(1)}, f32[128,128]{1,0:T(8,128)}, ...), branch_computations={%region_0.0_spmd, %region_1.0_spmd} | conditional | bytes 524324 | solution.py:853
  28.8 0.3 %target.2 = f32[2,256,256]{2,1,0:T(8,128)S(1)} custom-call(f32[256,128]{1,0:T(8,128)S(1)} %get-tuple-element.36.state_ref, f32[256,256]{1,0:T(8,128)S(1)} %get-tuple-element.37.cos_ref, f32[256,256]{1,0:T(8,128)S(1)} %get-tuple-element.38.sin_ref, bf16[384,512]{1,0:T(8,128)(2,1)S(1)} %get-tuple-element.39.table_ref), custom_call_target="tpu_custom_call" | custom-call | tf_op jit(solution)/shard_map/cond/branch_0_fun/target/pallas_call | solution.py:816
  29.1 0.0 copy-start.2
  29.2 0.8 %copy-done.2 = f32[2,256,256]{2,1,0:T(8,128)} copy-done((f32[2,256,256]{2,1,0:T(8,128)}, f32[2,256,256]{2,1,0:T(8,128)S(1)}, u32[]{:S(2)}) %copy-start.2) | copy-done | bytes 524312
Async XLA Ops:
  0.7 28.1 %copy-start.1 = (bf16[384,512]{1,0:T(8,128)(2,1)S(1)}, bf16[384,512]{1,0:T(8,128)(2,1)}, u32[]{:S(2)}) copy-start(bf16[384,512]{1,0:T(8,128)(2,1)} %constant.14.clone) | copy-start | bytes 1179652
  0.7 28.1 %copy-start.3 = (f32[128,2,128]{2,1,0:T(2,128)S(1)}, f32[128,2,128]{2,1,0:T(2,128)}, u32[]{:S(2)}) copy-start(f32[128,2,128]{2,1,0:T(2,128)} %param.13) | copy-start | bytes 393220
  0.7 28.1 %copy-start.4 = (f32[128,2,128]{2,1,0:T(2,128)S(1)}, f32[128,2,128]{2,1,0:T(2,128)}, u32[]{:S(2)}) copy-start(f32[128,2,128]{2,1,0:T(2,128)} %param.14) | copy-start | bytes 393220
  0.7 28.1 %copy-start.5 = (bf16[256,256]{1,0:T(8,128)(2,1)S(1)}, bf16[256,256]{1,0:T(8,128)(2,1)}, u32[]{:S(2)}) copy-start(bf16[256,256]{1,0:T(8,128)(2,1)} %constant.13.clone.w1_hbm) | copy-start | bytes 393220
  0.7 28.1 %copy-start.6 = (bf16[256,256]{1,0:T(8,128)(2,1)S(1)}, bf16[256,256]{1,0:T(8,128)(2,1)}, u32[]{:S(2)}) copy-start(bf16[256,256]{1,0:T(8,128)(2,1)} %constant.12.clone.w0_hbm) | copy-start | bytes 393220
  29.1 0.8 %copy-start.2 = (f32[2,256,256]{2,1,0:T(8,128)}, f32[2,256,256]{2,1,0:T(8,128)S(1)}, u32[]{:S(2)}) copy-start(f32[2,256,256]{2,1,0:T(8,128)S(1)} %get-tuple-element.63) | copy-start | bytes 1572868

commit v6 on v5

--- a/solution.py
+++ b/solution.py
@@ -652,10 +652,15 @@
     left = lax.broadcasted_iota(jnp.int32, (ndev, 128), 1) < 64
     cos_o = pltpu.roll(cos_p, 64, 1)
     sin_o = pltpu.roll(sin_p, 64, 1)
-    cos_s[0] = jnp.where(left, cos_p, cos_o)
-    cos_s[1] = jnp.where(left, cos_o, cos_p)
-    sin_s[0] = jnp.where(left, -sin_p, sin_o)
-    sin_s[1] = jnp.where(left, -sin_o, sin_p)
+    cos1 = [jnp.where(left, cos_p, cos_o), jnp.where(left, cos_o, cos_p)]
+    sin1 = [jnp.where(left, -sin_p, sin_o), jnp.where(left, -sin_o, sin_p)]
+    for jj in range(2):
+        cosv, sinv = cos1[jj], sin1[jj]
+        for step in range(dbits):
+            if step > 0:
+                cosv, sinv = cosv * cos1[jj] - sinv * sin1[jj], sinv * cos1[jj] + cosv * sin1[jj]
+            cos_s[step, jj] = cosv
+            sin_s[step, jj] = sinv
     second_all.wait_recv()
 
     meta = msg2_r[pl.ds(S2 - 1, nxy, stride=S2), :]
@@ -679,16 +684,12 @@
 
     sub = lax.broadcasted_iota(jnp.int32, (ndev // 8, 8, 128), 1)
     states = [state[0:ndev], state[ndev:lb]]
-    cosv = [cos_s[0], cos_s[1]]
-    sinv = [sin_s[0], sin_s[1]]
     for step in range(dbits):
         bit = 4 if step == 0 else (step - 1 if step <= 4 else step)
         w_ref = w0_ref if step % 2 == 0 else w1_ref
         for jj in range(2):
             state = states[jj]
-            if step > 0:
-                cosv[jj], sinv[jj] = (cosv[jj] * cos_s[jj] - sinv[jj] * sin_s[jj],
-                                      sinv[jj] * cos_s[jj] + cosv[jj] * sin_s[jj])
+            cosv, sinv = cos_s[step, jj], sin_s[step, jj]
             if bit < 3:
                 tiles = state.reshape(ndev // 8, 8, 128)
                 dist = 1 << bit
@@ -699,8 +700,8 @@
                 pairs = state.reshape(ndev >> (bit + 1), 2, 1 << bit, 128)
                 first = jnp.concatenate([pairs[:, 0:1], pairs[:, 0:1]], axis=1).reshape(ndev, 128)
                 second = jnp.concatenate([pairs[:, 1:2], pairs[:, 1:2]], axis=1).reshape(ndev, 128)
-            first = cosv[jj] * first + sinv[jj] * pltpu.roll(first, 64, 1)
-            second = cosv[jj] * second + sinv[jj] * pltpu.roll(second, 64, 1)
+            first = cosv * first + sinv * pltpu.roll(first, 64, 1)
+            second = cosv * second + sinv * pltpu.roll(second, 64, 1)
             high, low = split(jnp.concatenate([first, second], axis=1))
             main = jnp.dot(high, w_ref[...], preferred_element_type=F32)
             rest = jnp.dot(low, w_ref[:, 0:128], preferred_element_type=F32)
@@ -717,7 +718,7 @@
         return rcopy(ret_s.at[pl.ds(at * 2, 2)], ret_r.at[pl.ds(holder_at * 2, 2)], t_send, t_recv, (hi_to, lo_to))
 
     def send_eight(block, carry):
-        for a in range(1, 4):
+        for a in (2, 3, 1):
             for b in range(8):
                 ret_to(a, block * 8 + b).start()
         return carry
@@ -839,8 +840,8 @@
             pltpu.VMEM((nq * 64, 256), BF16),
             pltpu.VMEM((nxy * S2, 128), F32),
             pltpu.VMEM((nxy * S2, 128), F32),
-            pltpu.VMEM((2, lb // 2, 128), F32),
-            pltpu.VMEM((2, lb // 2, 128), F32),
+            pltpu.VMEM((7, 2, lb // 2, 128), F32),
+            pltpu.VMEM((7, 2, lb // 2, 128), F32),
             pltpu.VMEM((lb, 128), F32),
             pltpu.VMEM((lb, 128), F32),
             dma((9,)),

time: 30.1 us -> 30 us (level)
  no operation moved by 1% of the time
where the time goes in v6:
time: 30 us; the launch traced here: 29.8 us
  Pallas kernels  27.6 us (92%)
  between operations  1.39 us (5%)
  local copies, waits for them, and re-layouts  0.82 us (3%)
    pallas_call x1, Pallas kernels, local(): pl.pallas_call(slot_kernel, out_shape=(state_shape, jax.ShapeDtypeStruct(...  27.3 us
    unnamed x12, local copies, waits for them, and re-layouts  0.82 us

profile of v6, /device:TPU:1, one launch (start us, length us, event | category | flops | bytes accessed | tf_op | source)
XLA Modules:
  0.0 29.8 jit_solution(7635615040843044433)
XLA Ops:
  0.7 0.0 copy-start.1
  0.7 0.0 copy-start.3
  0.7 0.0 copy-start.4
  0.7 0.0 copy-start.5
  0.7 0.0 copy-start.6
  0.7 27.3 %slots.1 = (f32[256,128]{1,0:T(8,128)S(1)}, s32[1]{0:T(128)}, s32[1,128]{1,0:T(1,128)S(1)}, f32[256,256]{1,0:T(8,128)S(1)}, f32[256,256]{1,0:T(8,128)S(1)}) custom-call(f32[256,128]{1,0:T(8,128)} %bitcast.7, f32[256,128]{1,0:T(8,128)} %bitcast.9, f32[128,128]{1,0:T(8,128)} %phase_hbm.1, f32[64,256]{1,0:T(8,128)} %bitcast.11, ...), custom_call_target="tpu_custom_call" | custom-call | tf_op jit(solution)/shard_map/slots/pallas_call | solution.py:826
  28.7 0.0 copy-done.1
  28.7 0.0 copy-done.3
  28.7 0.0 copy-done.4
  28.7 0.0 copy-done.5
  28.7 0.0 copy-done.6
  28.7 0.3 %conditional.1 = (f32[2,256,256]{2,1,0:T(8,128)S(1)}) conditional(s32[]{:T(128)} %bitcast.5, (f32[256,128]{1,0:T(8,128)S(1)}, f32[256,256]{1,0:T(8,128)S(1)}, f32[256,256]{1,0:T(8,128)S(1)}, bf16[384,512]{1,0:T(8,128)(2,1)S(1)}) %tuple.17, (f32[256,128]{1,0:T(8,128)S(1)}, f32[256,128]{1,0:T(8,128)S(1)}, f32[128,128]{1,0:T(8,128)}, ...), branch_computations={%region_0.0_spmd, %region_1.0_spmd} | conditional | bytes 524324 | solution.py:854
  28.7 0.3 %target.2 = f32[2,256,256]{2,1,0:T(8,128)S(1)} custom-call(f32[256,128]{1,0:T(8,128)S(1)} %get-tuple-element.36.state_ref, f32[256,256]{1,0:T(8,128)S(1)} %get-tuple-element.37.cos_ref, f32[256,256]{1,0:T(8,128)S(1)} %get-tuple-element.38.sin_ref, bf16[384,512]{1,0:T(8,128)(2,1)S(1)} %get-tuple-element.39.table_ref), custom_call_target="tpu_custom_call" | custom-call | tf_op jit(solution)/shard_map/cond/branch_0_fun/target/pallas_call | solution.py:817
  29.0 0.0 copy-start.2
  29.1 0.8 %copy-done.2 = f32[2,256,256]{2,1,0:T(8,128)} copy-done((f32[2,256,256]{2,1,0:T(8,128)}, f32[2,256,256]{2,1,0:T(8,128)S(1)}, u32[]{:S(2)}) %copy-start.2) | copy-done | bytes 524312
Async XLA Ops:
  0.7 28.0 %copy-start.1 = (bf16[384,512]{1,0:T(8,128)(2,1)S(1)}, bf16[384,512]{1,0:T(8,128)(2,1)}, u32[]{:S(2)}) copy-start(bf16[384,512]{1,0:T(8,128)(2,1)} %constant.14.clone) | copy-start | bytes 1179652
  0.7 28.0 %copy-start.3 = (f32[128,2,128]{2,1,0:T(2,128)S(1)}, f32[128,2,128]{2,1,0:T(2,128)}, u32[]{:S(2)}) copy-start(f32[128,2,128]{2,1,0:T(2,128)} %param.13) | copy-start | bytes 393220
  0.7 28.0 %copy-start.4 = (f32[128,2,128]{2,1,0:T(2,128)S(1)}, f32[128,2,128]{2,1,0:T(2,128)}, u32[]{:S(2)}) copy-start(f32[128,2,128]{2,1,0:T(2,128)} %param.14) | copy-start | bytes 393220
  0.7 28.0 %copy-start.5 = (bf16[256,256]{1,0:T(8,128)(2,1)S(1)}, bf16[256,256]{1,0:T(8,128)(2,1)}, u32[]{:S(2)}) copy-start(bf16[256,256]{1,0:T(8,128)(2,1)} %constant.13.clone.w1_hbm) | copy-start | bytes 393220
  0.7 28.0 %copy-start.6 = (bf16[256,256]{1,0:T(8,128)(2,1)S(1)}, bf16[256,256]{1,0:T(8,128)(2,1)}, u32[]{:S(2)}) copy-start(bf16[256,256]{1,0:T(8,128)(2,1)} %constant.12.clone.w0_hbm) | copy-start | bytes 393220
  29.0 0.8 %copy-start.2 = (f32[2,256,256]{2,1,0:T(8,128)}, f32[2,256,256]{2,1,0:T(8,128)S(1)}, u32[]{:S(2)}) copy-start(f32[2,256,256]{2,1,0:T(8,128)S(1)} %get-tuple-element.63) | copy-start | bytes 1572868

commit v7 on v6

--- a/solution.py
+++ b/solution.py
@@ -463,8 +463,7 @@
 
 
 XY_STEPS = sorted(range(1, 16), key=lambda s: -far(s // 4, 4) - far(s % 4, 4))
-Q_STEPS = sorted(range(1, 8), key=lambda s: -far(s // 4 * 2 + s % 2, 4))
-ALL_STEPS = sorted(range(1, 128), key=lambda s: -far(s // 64 * 2 + s % 2, 4) - far(s // 8 % 4, 4) - far(s // 2 % 4, 4))
+Q_STEPS = sorted(range(1, 8), key=lambda s: far(s // 4 * 2 + s % 2, 4))
 
 
 def nt_dot(left, right):

time: 30 us -> 29.5 us (0.983)
  Pallas kernels: 27.6 us -> 27.2 us
    pallas_call x1, Pallas kernels: 27.3 us -> 26.9 us  [local(): pl.pallas_call(slot_kernel, out_shape=(state_shape, jax.ShapeDtypeStruct(...]
where the time goes in v7:
time: 29.5 us; the launch traced here: 29.4 us
  Pallas kernels  27.2 us (92%)
  between operations  1.39 us (5%)
  local copies, waits for them, and re-layouts  0.82 us (3%)
    pallas_call x1, Pallas kernels, local(): pl.pallas_call(slot_kernel, out_shape=(state_shape, jax.ShapeDtypeStruct(...  26.9 us
    unnamed x12, local copies, waits for them, and re-layouts  0.82 us

profile of v7, /device:TPU:1, one launch (start us, length us, event | category | flops | bytes accessed | tf_op | source)
XLA Modules:
  0.0 29.4 jit_solution(14133311158867751366)
XLA Ops:
  0.7 0.0 copy-start.1
  0.7 0.0 copy-start.3
  0.7 0.0 copy-start.4
  0.7 0.0 copy-start.5
  0.7 0.0 copy-start.6
  0.7 26.9 %slots.1 = (f32[256,128]{1,0:T(8,128)S(1)}, s32[1]{0:T(128)}, s32[1,128]{1,0:T(1,128)S(1)}, f32[256,256]{1,0:T(8,128)S(1)}, f32[256,256]{1,0:T(8,128)S(1)}) custom-call(f32[256,128]{1,0:T(8,128)} %bitcast.7, f32[256,128]{1,0:T(8,128)} %bitcast.9, f32[128,128]{1,0:T(8,128)} %phase_hbm.1, f32[64,256]{1,0:T(8,128)} %bitcast.11, ...), custom_call_target="tpu_custom_call" | custom-call | tf_op jit(solution)/shard_map/slots/pallas_call | solution.py:825
  28.2 0.0 copy-done.1
  28.2 0.0 copy-done.3
  28.2 0.0 copy-done.4
  28.3 0.0 copy-done.5
  28.3 0.0 copy-done.6
  28.3 0.3 %conditional.1 = (f32[2,256,256]{2,1,0:T(8,128)S(1)}) conditional(s32[]{:T(128)} %bitcast.5, (f32[256,128]{1,0:T(8,128)S(1)}, f32[256,256]{1,0:T(8,128)S(1)}, f32[256,256]{1,0:T(8,128)S(1)}, bf16[384,512]{1,0:T(8,128)(2,1)S(1)}) %tuple.17, (f32[256,128]{1,0:T(8,128)S(1)}, f32[256,128]{1,0:T(8,128)S(1)}, f32[128,128]{1,0:T(8,128)}, ...), branch_computations={%region_0.0_spmd, %region_1.0_spmd} | conditional | bytes 524324 | solution.py:853
  28.3 0.3 %target.2 = f32[2,256,256]{2,1,0:T(8,128)S(1)} custom-call(f32[256,128]{1,0:T(8,128)S(1)} %get-tuple-element.36.state_ref, f32[256,256]{1,0:T(8,128)S(1)} %get-tuple-element.37.cos_ref, f32[256,256]{1,0:T(8,128)S(1)} %get-tuple-element.38.sin_ref, bf16[384,512]{1,0:T(8,128)(2,1)S(1)} %get-tuple-element.39.table_ref), custom_call_target="tpu_custom_call" | custom-call | tf_op jit(solution)/shard_map/cond/branch_0_fun/target/pallas_call | solution.py:816
  28.6 0.0 copy-start.2
  28.6 0.8 %copy-done.2 = f32[2,256,256]{2,1,0:T(8,128)} copy-done((f32[2,256,256]{2,1,0:T(8,128)}, f32[2,256,256]{2,1,0:T(8,128)S(1)}, u32[]{:S(2)}) %copy-start.2) | copy-done | bytes 524312
Async XLA Ops:
  0.7 27.6 %copy-start.1 = (bf16[384,512]{1,0:T(8,128)(2,1)S(1)}, bf16[384,512]{1,0:T(8,128)(2,1)}, u32[]{:S(2)}) copy-start(bf16[384,512]{1,0:T(8,128)(2,1)} %constant.14.clone) | copy-start | bytes 1179652
  0.7 27.6 %copy-start.3 = (f32[128,2,128]{2,1,0:T(2,128)S(1)}, f32[128,2,128]{2,1,0:T(2,128)}, u32[]{:S(2)}) copy-start(f32[128,2,128]{2,1,0:T(2,128)} %param.13) | copy-start | bytes 393220
  0.7 27.6 %copy-start.4 = (f32[128,2,128]{2,1,0:T(2,128)S(1)}, f32[128,2,128]{2,1,0:T(2,128)}, u32[]{:S(2)}) copy-start(f32[128,2,128]{2,1,0:T(2,128)} %param.14) | copy-start | bytes 393220
  0.7 27.6 %copy-start.5 = (bf16[256,256]{1,0:T(8,128)(2,1)S(1)}, bf16[256,256]{1,0:T(8,128)(2,1)}, u32[]{:S(2)}) copy-start(bf16[256,256]{1,0:T(8,128)(2,1)} %constant.13.clone.w1_hbm) | copy-start | bytes 393220
  0.7 27.6 %copy-start.6 = (bf16[256,256]{1,0:T(8,128)(2,1)S(1)}, bf16[256,256]{1,0:T(8,128)(2,1)}, u32[]{:S(2)}) copy-start(bf16[256,256]{1,0:T(8,128)(2,1)} %constant.12.clone.w0_hbm) | copy-start | bytes 393220
  28.6 0.8 %copy-start.2 = (f32[2,256,256]{2,1,0:T(8,128)}, f32[2,256,256]{2,1,0:T(8,128)S(1)}, u32[]{:S(2)}) copy-start(f32[2,256,256]{2,1,0:T(8,128)S(1)} %get-tuple-element.63) | copy-start | bytes 1572868
